TPU v7x, 128 devices: a whole 4x4x4 slice. The times are simulated.
128 devices in a mesh: head: 8 (over z_lo, y), resp: 16 (over z_hi, x, core).
Axes of the slice: x: 4, y: 4, z: 4 (z_hi: 2, z_lo: 2; z = z_hi * 2 + z_lo), core: 2. Of those that a mesh axis runs over, the one named last changes fastest.
Arguments:
- queries: bfloat16 [16, 128, 64, 128], P('resp', None, 'head'), may hold values from -8 to 8
- resp_keys: bfloat16 [16, 128, 8, 128], P('resp', None, 'head'), may hold values from -6 to 6
- resp_values: bfloat16 [16, 128, 8, 128], P('resp', None, 'head'), may hold values from -6 to 6
- out_grad: bfloat16 [16, 128, 64, 128], P('resp', None, 'head'), may hold values from -6 to 6
- prefix_keys: bfloat16 [8192, 8, 128], P('resp', 'head'), may hold values from -4 to 4
- prefix_values: bfloat16 [8192, 8, 128], P('resp', 'head'), may hold values from -6 to 6
- w_query: bfloat16 [5120, 8192], P(None, 'head'), may hold values from -0.0625 to 0.0625
- w_key: bfloat16 [5120, 1024], P(None, 'head'), may hold values from -0.1875 to 0.1875
- w_value: bfloat16 [5120, 1024], P(None, 'head'), may hold values from -0.1875 to 0.1875
- resp_lengths: int32 [16], replicated, may hold values from 1 to 128, 1280 in all
Outputs:
- d_hidden: bfloat16 [16, 128, 5120], P('resp', 'head')
- prefix_dk: bfloat16 [8192, 8, 128], P('resp', 'head')
- prefix_dv: bfloat16 [8192, 8, 128], P('resp', 'head')
Inputs may be any that keep to these rules, and one draw needn't show every extreme that they name: `resp_lengths`: some response has all 128 rows live.
All inputs are finite; a program needn't handle non-finite values.
Results may differ from a plain program's by a relative error of at most 0.019.
Values may be sent and summed in bfloat16 or wider, within the bound.
A program may use at most 128 MiB of HBM per device.

v0:
```python
import math

import jax
import jax.numpy as jnp
from jax import lax
from jax.sharding import PartitionSpec as P

NEG = -1e30


def per_device(
    queries,
    resp_keys,
    resp_values,
    out_grad,
    prefix_keys,
    prefix_values,
    w_query,
    w_key,
    w_value,
    resp_lengths,
):
    row_count = queries.shape[1]
    heads_here = queries.shape[2]
    head_size = queries.shape[3]
    kv_here = resp_keys.shape[2]
    group_size = heads_here // kv_here
    scaling = head_size ** (-0.5)
    live_length = lax.dynamic_index_in_dim(resp_lengths, lax.axis_index("resp"), 0, keepdims=False)
    is_live = jnp.arange(row_count, dtype=jnp.int32) < live_length
    live_grad = jnp.where(is_live[:, None, None], out_grad[0], jnp.zeros_like(out_grad[0]))
    query_rows = queries[0].reshape(row_count, kv_here, group_size, head_size)
    grad_rows = live_grad.reshape(row_count, kv_here, group_size, head_size)
    self_keys = resp_keys[0]
    self_values = resp_values[0]
    causal = jnp.arange(row_count)[None, :] <= jnp.arange(row_count)[:, None]
    stat_shape = (kv_here, group_size, row_count)
    gathered_keys, gathered_values = (
        lax.all_gather(prefix_keys, "resp", axis=0, tiled=True),
        lax.all_gather(prefix_values, "resp", axis=0, tiled=True),
    )
    tile_rows = math.gcd(gathered_keys.shape[0], 512)
    tile_count = gathered_keys.shape[0] // tile_rows
    key_tiles = gathered_keys.reshape(tile_count, tile_rows, kv_here, head_size)
    value_tiles = gathered_values.reshape(tile_count, tile_rows, kv_here, head_size)

    def logits(query_part, key_tile, allowed):
        scores = (
            jnp.einsum("rcgd,kcd->cgrk", query_part, key_tile, preferred_element_type=jnp.float32)
            * scaling
        )
        if allowed is None:
            return scores
        return jnp.where(allowed[None, None], scores, NEG)

    def running_total(folded, key_tile, allowed):
        highest, totals = folded
        scores = logits(query_rows, key_tile, allowed)
        new_high = jnp.maximum(highest, jnp.max(scores, -1))
        totals = totals * jnp.exp(highest - new_high) + jnp.sum(
            jnp.exp(scores - new_high[..., None]), -1
        )
        return (new_high, totals)

    start_stats = (jnp.full(stat_shape, NEG, jnp.float32), jnp.zeros(stat_shape, jnp.float32))
    folded, _ = lax.scan(
        lambda carry_in, key_tile: (running_total(carry_in, key_tile, None), None),
        start_stats,
        key_tiles,
    )
    highest, totals = running_total(folded, self_keys, causal)
    log_total = highest + jnp.log(totals)

    def weights(key_tile, value_tile, allowed):
        attend = jnp.exp(logits(query_rows, key_tile, allowed) - log_total[..., None])
        attend_b = attend.astype(jnp.bfloat16)
        pulled = jnp.einsum(
            "rcgd,kcd->cgrk", grad_rows, value_tile, preferred_element_type=jnp.float32
        )
        return (attend, attend_b, pulled)

    def delta_step(running, tiles):
        attend, attend_b, pulled = weights(tiles[0], tiles[1], None)
        return (running + jnp.sum(attend_b.astype(jnp.float32) * pulled, -1), None)

    row_delta, _ = lax.scan(
        delta_step, jnp.zeros(stat_shape, jnp.float32), (key_tiles, value_tiles)
    )
    attend, attend_b, pulled = weights(self_keys, self_values, causal)
    row_delta = row_delta + jnp.sum(attend_b.astype(jnp.float32) * pulled, -1)

    def gradients(key_tile, value_tile, allowed):
        attend, attend_b, pulled = weights(key_tile, value_tile, allowed)
        slope = (attend * (pulled - row_delta[..., None])).astype(jnp.bfloat16)
        query_part = jnp.einsum(
            "cgrk,kcd->rcgd", slope, key_tile, preferred_element_type=jnp.float32
        )
        key_part = (
            jnp.einsum("cgrk,rcgd->kcd", slope, query_rows, preferred_element_type=jnp.float32)
            * scaling
        )
        value_part = jnp.einsum(
            "cgrk,rcgd->kcd", attend_b, grad_rows, preferred_element_type=jnp.float32
        )
        return (query_part, key_part, value_part)

    query_zero = jnp.zeros((row_count, kv_here, group_size, head_size), jnp.float32)

    def grad_step(running, tiles):
        query_part, key_part, value_part = gradients(tiles[0], tiles[1], None)
        return (running + query_part, (key_part, value_part))

    query_accum, (key_parts, value_parts) = lax.scan(
        grad_step, query_zero, (key_tiles, value_tiles)
    )
    summed_k, summed_v = (
        lax.psum_scatter(
            key_parts.reshape(gathered_keys.shape).astype(jnp.bfloat16),
            "resp",
            scatter_dimension=0,
            tiled=True,
        ).astype(jnp.float32),
        lax.psum_scatter(
            value_parts.reshape(gathered_values.shape).astype(jnp.bfloat16),
            "resp",
            scatter_dimension=0,
            tiled=True,
        ).astype(jnp.float32),
    )
    query_self, key_self, value_self = gradients(self_keys, self_values, causal)
    query_flat = (
        ((query_accum + query_self) * scaling)
        .astype(jnp.bfloat16)
        .reshape(row_count, heads_here * head_size)
    )
    key_flat = key_self.astype(jnp.bfloat16).reshape(row_count, kv_here * head_size)
    value_flat = value_self.astype(jnp.bfloat16).reshape(row_count, kv_here * head_size)
    row_share = row_count // lax.axis_size("head")
    query_part = query_flat
    key_part = key_flat
    value_part = value_flat
    partial_value = jnp.einsum("rf,df->rd", query_part, w_query, preferred_element_type=jnp.float32)
    partial_value = partial_value + jnp.einsum(
        "rf,df->rd", key_part, w_key, preferred_element_type=jnp.float32
    )
    summed_hidden = lax.psum_scatter(
        (
            partial_value
            + jnp.einsum("rf,df->rd", value_part, w_value, preferred_element_type=jnp.float32)
        ).astype(jnp.bfloat16),
        "head",
        scatter_dimension=0,
        tiled=True,
    ).astype(jnp.float32)
    d_hidden = summed_hidden.astype(jnp.bfloat16).reshape(1, row_share, summed_hidden.shape[1])
    return (d_hidden, summed_k.astype(jnp.bfloat16), summed_v.astype(jnp.bfloat16))


def solution(mesh):
    in_specs = (
        P("resp", None, "head", None),
        P("resp", None, "head", None),
        P("resp", None, "head", None),
        P("resp", None, "head", None),
        P("resp", "head", None),
        P("resp", "head", None),
        P(None, "head"),
        P(None, "head"),
        P(None, "head"),
        P(),
    )
    out_specs = (P("resp", "head", None), P("resp", "head", None), P("resp", "head", None))
    return jax.shard_map(
        per_device, mesh=mesh, in_specs=in_specs, out_specs=out_specs, check_vma=False
    )
```

profile of v0, /device:TPU:1, one launch (start us, length us, event | category | flops | bytes accessed | tf_op | source)
XLA Modules:
  0.0 517.3 jit_solution(12316199291015295799)
XLA Ops:
  10.7 1.9 select_bitcast_fusion
  12.5 1.7 bitcast_select_fusion.3
  14.3 1.7 copy.45
  16.0 2.0 fusion.78
  18.0 44.6 %all-gather.3.cloned.1.call-done = bf16[8192,1,128]{2,0,1:T(8,128)(2,1)} async-done(((bf16[512,1,128]{2,0,1:T(8,128)(2,1)}), bf16[8192,1,128]{2,0,1:T(8,128)(2,1)}) %all-gather.3.cloned.1.call-update) | async-done | bytes 2097168 | tf_op jit(solution)/shard_map/all_gather | solution.py:39
  62.5 30.3 %while.39 = (s32[]{:T(128)}, f32[1,8,128]{2,1,0:T(8,128)S(1)}, f32[1,8,128]{2,1,0:T(8,128)S(1)}, bf16[16,512,1,128]{3,1,2,0:T(8,128)(2,1)}, bf16[128,1,8,128]{3,0,2,1:T(8,128)(2,1)}, /*index=5*/s32[]{:T(128)}, s32[]{:T(128)}) while((s32[]{:T(128)}, f32[1,8,128]{2,1,0:T(8,128)S(1)}, f32[1,8,128]{2,1,0:T(8,128)S(1)}, ...), condition=%wide.region_3.4_spmd.clone, body=%wide.region_0.3_spmd.clone.sunk | while | flops 136844288 | bytes 4641368 | solution.py:66
  94.2 17.9 %all-gather.5.cloned.1.call-done = bf16[8192,1,128]{2,0,1:T(8,128)(2,1)} async-done(((bf16[512,1,128]{2,0,1:T(8,128)(2,1)}), bf16[8192,1,128]{2,0,1:T(8,128)(2,1)}) %all-gather.5.cloned.1.call-update) | async-done | bytes 2097168 | tf_op jit(solution)/shard_map/all_gather | solution.py:40
  112.1 49.4 %while.40 = (s32[]{:T(128)}, f32[1,8,128]{2,1,0:T(8,128)S(1)}, bf16[16,512,1,128]{3,1,2,0:T(8,128)(2,1)}, bf16[128,1,8,128]{3,0,2,1:T(8,128)(2,1)}, f32[1,8,128]...) while((s32[]{:T(128)}, f32[1,8,128]{2,1,0:T(8,128)S(1)}, ...), condition=%wide.region_8.9_spmd.clone, body=%wide.region_6.8_spmd.clone.sunk | while | flops 271582208 | bytes 2905191 | solution.py:86
  112.1 1.6 fusion.116
  115.3 1.6 fusion.116
  118.3 1.6 fusion.116
  121.4 1.6 fusion.116
  124.5 1.6 fusion.116
  127.6 1.6 fusion.116
  130.7 1.6 fusion.116
  133.7 1.6 fusion.116
  136.8 1.6 fusion.116
  139.9 1.6 fusion.116
  143.0 1.6 fusion.116
  146.1 1.6 fusion.116
  149.2 1.6 fusion.116
  152.2 1.6 fusion.116
  155.3 1.6 fusion.116
  158.4 1.6 fusion.116
  162.5 143.6 %while.41 = (s32[]{:T(128)}, f32[128,1,8,128]{0,3,2,1:T(8,128)}, bf16[16,512,1,128]{3,1,2,0:T(8,128)(2,1)}, bf16[16,512,1,128]{3,1,2,0:T(8,128)(2,1)}, bf16[16,5...) while((s32[]{:T(128)}, f32[128,1,8,128]{0,3,2,1:T(8,128)}, ...), condition=%wide.region_11.12_spmd.clone, body=%wide.region_10.11_spmd.clone.sunk | while | flops 675610624 | bytes 19806960 | solution.py:113
  167.8 2.5 fusion.130
  176.6 2.6 fusion.130
  185.6 2.6 fusion.130
  194.6 2.6 fusion.130
  203.6 2.6 fusion.130
  212.5 2.6 fusion.130
  217.8 1.6 fusion.129
  221.5 2.6 fusion.130
  230.5 2.6 fusion.130
  239.5 2.6 fusion.130
  248.5 2.6 fusion.130
  257.5 2.6 fusion.130
  266.5 2.6 fusion.130
  275.4 2.6 fusion.130
  284.4 2.6 fusion.130
  293.4 2.6 fusion.130
  302.4 2.6 fusion.130
  308.8 9.2 %fusion.79 = f32[128,5120]{1,0:T(8,128)} fusion(bf16[128,1024]{0,1:T(8,128)(2,1)S(1)} %bitcast.341, bf16[5120,1024]{1,0:T(8,128)(2,1)} %param.22), kind=kOutput, calls=%fused_computation.107 | convolution fusion | flops 1342177280 | bytes 13369344 | tf_op jit(solution)/shard_map/rf,df->rd/dot_general | solution.py:142
  318.0 4.0 convolution_add_fusion.1
  322.0 3.8 fusion.47
  327.1 32.2 %reduce-scatter.4.cloned.1.call-done = bf16[16,5120]{1,0:T(8,128)(2,1)} async-done(((bf16[128,5120]{1,0:T(8,128)(2,1)}), bf16[16,5120]{1,0:T(8,128)(2,1)}) %reduce-scatter.4.cloned.1.call-update) | async-done | bytes 163856 | tf_op jit(solution)/shard_map/reduce_scatter | solution.py:146
  359.3 77.2 %reduce-scatter.6.cloned.1.call-done = bf16[512,1,128]{2,0,1:T(8,128)(2,1)} async-done(((bf16[8192,1,128]{2,0,1:T(8,128)(2,1)}), bf16[512,1,128]{2,0,1:T(8,128)(2,1)}) %reduce-scatter.6.cloned.1.call-update) | async-done | bytes 131088 | tf_op jit(solution)/shard_map/reduce_scatter | solution.py:117
  436.4 74.3 %reduce-scatter.8.cloned.1.call-done = bf16[512,1,128]{2,0,1:T(8,128)(2,1)} async-done(((bf16[8192,1,128]{2,0,1:T(8,128)(2,1)}), bf16[512,1,128]{2,0,1:T(8,128)(2,1)}) %reduce-scatter.8.cloned.1.call-update) | async-done | bytes 131088 | tf_op jit(solution)/shard_map/reduce_scatter | solution.py:123
  (348 shorter events, 162.2 us)
Async XLA Ops:
  7.2 310.8 %copy-start = (bf16[5120,128]{1,0:T(8,128)(2,1)S(1)}, bf16[5120,128]{1,0:T(8,128)(2,1)}, u32[]{:S(2)}) copy-start(bf16[5120,128]{1,0:T(8,128)(2,1)} %param.23) | copy-start | bytes 3932164
  7.2 55.4 %all-gather.3.cloned.1.call-start = ((), (), s32[]{:S(2)}) async-start(), calls=%async_computation.3 | async-start | bytes 2228224 | tf_op jit(solution)/shard_map/all_gather | solution.py:39
  7.9 104.2 %all-gather.5.cloned.1.call-start = ((), (), s32[]{:S(2)}) async-start(), calls=%async_computation.4 | async-start | bytes 2228224 | tf_op jit(solution)/shard_map/all_gather | solution.py:40
  8.7 350.6 %reduce-scatter.4.cloned.1.call-start = ((), (), s32[]{:S(2)}) async-start(), calls=%async_computation.5 | async-start | bytes 1474560 | tf_op jit(solution)/shard_map/reduce_scatter | solution.py:146
  112.1 49.4 %copy-start.6 = (f32[1,8,128,128]{2,3,1,0:T(8,128)S(1)}, f32[1,8,128,128]{2,3,1,0:T(8,128)}, u32[]{:S(2)}) copy-start(f32[1,8,128,128]{2,3,1,0:T(8,128)} %get-tuple-element.252) | copy-start | bytes 1572868
  112.1 49.4 %copy-start.10 = (bf16[128,8,128]{2,1,0:T(8,128)(2,1)S(1)}, bf16[128,8,128]{2,1,0:T(8,128)(2,1)}, u32[]{:S(2)}) copy-start(bf16[128,8,128]{2,1,0:T(8,128)(2,1)} %select_bitcast_fusion) | copy-start | bytes 786436
  112.1 49.4 %copy-start.12 = (bf16[1,128,1,128]{3,1,2,0:T(8,128)(2,1)S(1)}, bf16[1,128,1,128]{3,1,2,0:T(8,128)(2,1)}, u32[]{:S(2)}) copy-start(bf16[1,128,1,128]{3,1,2,0:T(8,128)(2,1)} %param.18) | copy-start | bytes 98308
  164.0 2.6 copy-start.2
  167.8 2.5 copy-start.4
  172.9 2.6 copy-start.2
  176.6 2.6 copy-start.4
  180.4 1.5 copy-start.3
  181.9 2.6 copy-start.2
  185.6 2.6 copy-start.4
  190.9 2.6 copy-start.2
  194.6 2.6 copy-start.4
  198.4 1.5 copy-start.3
  199.8 2.6 copy-start.2
  203.6 2.6 copy-start.4
  208.8 2.6 copy-start.2
  212.5 2.6 copy-start.4
  217.8 2.6 copy-start.2
  221.5 2.6 copy-start.4
  226.8 2.6 copy-start.2
  230.5 2.6 copy-start.4
  235.8 2.6 copy-start.2
  239.5 2.6 copy-start.4
  244.8 2.6 copy-start.2
  248.5 2.6 copy-start.4
  253.8 2.6 copy-start.2
  257.5 2.6 copy-start.4
  262.7 2.6 copy-start.2
  266.5 2.6 copy-start.4
  271.7 2.6 copy-start.2
  275.4 2.6 copy-start.4
  280.7 2.6 copy-start.2
  284.4 2.6 copy-start.4
  289.7 2.6 copy-start.2
  293.4 2.6 copy-start.4
  298.7 2.6 copy-start.2
  302.4 2.6 copy-start.4
  306.2 2.3 copy-start.5
  306.2 2.3 copy-start.11
  308.7 9.2 %copy-start.7 = (bf16[1,128,8,128]{3,2,1,0:T(8,128)(2,1)S(1)}, bf16[1,128,8,128]{3,2,1,0:T(8,128)(2,1)}, u32[]{:S(2)}) copy-start(bf16[1,128,8,128]{3,2,1,0:T(8,128)(2,1)} %param.16) | copy-start | bytes 786436
  318.0 4.1 copy-start.8
  318.0 4.1 copy-start.9
  325.9 110.5 %reduce-scatter.6.cloned.1.call-start = ((), (), s32[]{:S(2)}) async-start(), calls=%async_computation.6 | async-start | bytes 2228224 | tf_op jit(solution)/shard_map/reduce_scatter | solution.py:117
  326.5 184.3 %reduce-scatter.8.cloned.1.call-start = ((), (), s32[]{:S(2)}) async-start(), calls=%async_computation.7 | async-start | bytes 2228224 | tf_op jit(solution)/shard_map/reduce_scatter | solution.py:123
  (30 other events, 38.0 us)
Sparse Core Ops, SparseCore 0:
  10.5 52.0 all-gather.2
  65.0 47.0 all-gather.4
  326.0 33.2 reduce-scatter.3
  363.6 72.7 reduce-scatter.5
  440.8 69.8 reduce-scatter.7
where the time goes:
time: 521 us; the launch traced here: 517 us
  waiting for transfers between devices  249 us (48%)
  matrix products  218 us (42%)
  local copies, waits for them, and re-layouts  20.9 us (4%)
  between operations  13.9 us (3%)
  other arithmetic  13.1 us (3%)
    reduce_scatter x1, waiting for transfers between devices, per_device(): lax.psum_scatter(key_parts.reshape(gathered_keys.shape).astype(jnp.bfloat...  77.2 us
    dot_general x49, matrix products, logits(): jnp.einsum('rcgd,kcd->cgrk', query_part, key_tile, preferred_element_type...  74.4 us
    reduce_scatter x1, waiting for transfers between devices, per_device(): lax.psum_scatter(value_parts.reshape(gathered_values.shape).astype(jnp.bf...  74.3 us
    dot_general x33, matrix products, weights(): jnp.einsum('rcgd,kcd->cgrk', grad_rows, value_tile, preferred_element_typ...  49.2 us
    all_gather x1, waiting for transfers between devices, per_device(): lax.all_gather(prefix_keys, 'resp', axis=0, tiled=True)  44.6 us
    dot_general x17, matrix products, gradients(): jnp.einsum('cgrk,kcd->rcgd', slope, key_tile, preferred_element_type=jnp....  42 us
    reduce_scatter x1, waiting for transfers between devices, per_device(): lax.psum_scatter((partial_value + jnp.einsum('rf,df->rd', value_part, w_v...  32.2 us
    dot_general x16, matrix products, gradients(): jnp.einsum('cgrk,rcgd->kcd', attend_b, grad_rows, preferred_element_type=...  18.2 us
  transfers between devices with their start and end apart: 5, of which 5 were waited for; matrix products, arithmetic and copies ran while one was open for 8% of the time, Pallas kernels for 0%

commit v1 on v0

v1 whole, which is shorter than its diff:
```python
import functools
import math

import jax
import jax.numpy as jnp
from jax import lax
from jax.experimental import pallas as pl
from jax.experimental.pallas import tpu as pltpu
from jax.sharding import PartitionSpec as P

MESH = pl.DeviceIdType.MESH
NT = (((1,), (1,)), ((), ()))
F32, BF16 = jnp.float32, jnp.bfloat16
PLACES = ((0, 0), (0, 1), (0, 3), (1, 0), (0, 2), (1, 1), (1, 3), (1, 2))
BACK = (0, 2, 1, 3, 4, 6, 5, 7)
BLOCKS = 8
SHARE = 512
CHUNK = 512
SLOTS = 4


def kernel(
    lengths, q_hbm, g_hbm, rk_hbm, rv_hbm, k_hbm, v_hbm, wq_hbm, wk_hbm, wv_hbm,
    hidden_out, dk_out, dv_out,
    q_all, g_all, k_all, v_all, q_scaled, k_turned, prob, grad, top, total, mean,
    log_total, delta, rk, rv, causal_p, causal_d, causal_stat, stat_own, stat_in,
    dq_turned, dq_in, dq_rows, flat, weight, hid, hid_in, own, dk_in, dv_in,
    local_sem, weight_sem, q_send, q_recv, k_send, k_recv, v_send, v_recv,
    stat_send, stat_recv, dq_send, dq_recv, dk_send, dk_recv, dv_send, dv_recv, hid_send, hid_recv,
):
    rows = q_all.shape[1]
    self_rows = rk.shape[0]
    group = rows // self_rows
    head = lax.axis_index("head")
    resp = lax.axis_index("resp")
    z_lo, y = head // 4, head % 4
    z_hi, x, core = resp // 8, (resp // 2) % 4, resp % 2
    scaling = q_all.shape[2] ** -0.5
    log2e = math.log2(math.e)
    chunks = hid.shape[1] // CHUNK

    def class_mate(n):
        dz, dx = PLACES[n]
        return (head, ((z_hi + dz) % 2) * 8 + ((x + dx) % 4) * 2 + core)

    sibling = (head, z_hi * 8 + x * 2 + (1 - core))

    def head_index(e):
        return ((z_lo + e // 4) % 2) * 4 + (y + e % 4) % 4

    def local(i, source, target):
        return pltpu.make_async_copy(source, target, local_sem.at[i])

    loads = [
        local(0, k_hbm, k_all.at[pl.ds(0, SHARE), :]),
        local(1, v_hbm, v_all.at[pl.ds(0, SHARE), :]),
        local(2, q_hbm, q_all.at[0]),
        local(3, g_hbm, g_all.at[0]),
        local(4, rk_hbm, rk),
        local(5, rv_hbm, rv),
    ]
    for load in loads:
        load.start()

    def weight_loads(c, slot):
        piece = pl.ds(pl.multiple_of(c * CHUNK, CHUNK), CHUNK)
        wide = q_all.shape[2]
        width = group * wide
        return [
            pltpu.make_async_copy(wq_hbm.at[piece, :], weight.at[slot, :, pl.ds(0, width)], weight_sem.at[slot, 0]),
            pltpu.make_async_copy(wk_hbm.at[piece, :], weight.at[slot, :, pl.ds(width, wide)], weight_sem.at[slot, 1]),
            pltpu.make_async_copy(
                wv_hbm.at[piece, :], weight.at[slot, :, pl.ds(width + wide, wide)], weight_sem.at[slot, 2]
            ),
        ]

    barrier = pltpu.get_barrier_semaphore()
    partners = [class_mate(n) for n in range(1, BLOCKS)] + [sibling] + [(head_index(e), resp) for e in range(1, 8)]
    for partner in partners:
        pl.semaphore_signal(barrier, inc=1, device_id=partner, device_id_type=MESH)

    for load in loads:
        load.wait()
    place = lax.broadcasted_iota(jnp.int32, (rows, 1), 0)
    live = place < lengths[resp] * group
    g_all[0] = jnp.where(live, g_all[0], jnp.zeros_like(g_all[0]))

    pl.semaphore_wait(barrier, len(partners))

    def remote(source, target, send, recv, device):
        return pltpu.make_async_remote_copy(
            src_ref=source, dst_ref=target, send_sem=send, recv_sem=recv, device_id=device, device_id_type=MESH
        )

    pair = [
        remote(q_all.at[0], q_all.at[1], q_send.at[0], q_recv.at[0], sibling),
        remote(g_all.at[0], g_all.at[1], q_send.at[1], q_recv.at[1], sibling),
    ]
    for copy in pair:
        copy.start()

    def block(n):
        return pl.ds(pl.multiple_of(n * SHARE, SHARE), SHARE)

    shares = []
    for n in range(1, BLOCKS):
        there = pl.ds(BACK[n] * SHARE, SHARE)
        here = pl.ds(0, SHARE)
        for held, send, recv in ((k_all, k_send, k_recv), (v_all, v_send, v_recv)):
            copy = remote(held.at[here, :], held.at[there, :], send.at[n], recv.at[BACK[n]], class_mate(n))
            copy.start()
            shares.append(copy)
    for c in range(SLOTS):
        for load in weight_loads(c, c):
            load.start()

    def scale_queries(slot):
        exact = q_all[slot].astype(F32) * (scaling * log2e)
        high = exact.astype(BF16)
        q_scaled[slot, :, : q_all.shape[2]] = high
        q_scaled[slot, :, q_all.shape[2] :] = (exact - high.astype(F32)).astype(BF16)

    def first_pass(keys, values, slot, allowed):
        twice = jnp.concatenate([keys, keys], axis=1)
        scores = lax.dot_general(twice, q_scaled[slot], NT, preferred_element_type=F32)
        if allowed is not None:
            scores = jnp.where(allowed, scores, -1e30)
        pulled = lax.dot_general(values, g_all[slot], NT, preferred_element_type=F32)
        high = jnp.max(scores, axis=0, keepdims=True)
        weights = jnp.exp2(scores - high)
        amount = jnp.sum(weights, axis=0, keepdims=True)
        centre = jnp.sum(weights * pulled, axis=0, keepdims=True) / amount
        return weights.astype(BF16), (pulled - centre).astype(BF16), high, amount, centre

    scale_queries(0)
    key_place = lax.broadcasted_iota(jnp.int32, (self_rows, rows), 0)
    row_place = lax.broadcasted_iota(jnp.int32, (self_rows, rows), 1) // group
    causal_p[...], causal_d[...], high, amount, centre = first_pass(rk[...], rv[...], 0, key_place <= row_place)
    causal_stat[0], causal_stat[1], causal_stat[2] = high, amount, centre
    for copy in pair:
        copy.wait_recv()
    scale_queries(1)

    def score_block(n, carry):
        here = block(n)

        @pl.when(n > 0)
        def _():
            for held, send, recv in ((k_all, k_send, k_recv), (v_all, v_send, v_recv)):
                remote(held.at[here, :], held.at[here, :], send.at[n], recv.at[n], sibling).wait_recv()

        keys, values = k_all[here, :], v_all[here, :]
        k_turned[:, here] = keys.T
        for slot in range(2):
            mine = pl.ds(slot * rows, rows)
            prob[here, mine], grad[here, mine], high, amount, centre = first_pass(keys, values, slot, None)
            top[n, :, mine] = high
            total[n, :, mine] = amount
            mean[n, :, mine] = centre
        return carry

    lax.fori_loop(0, BLOCKS, score_block, 0)

    for slot in range(2):
        mine = pl.ds(slot * rows, rows)
        high = top[0, :, mine]
        for n in range(1, BLOCKS):
            high = jnp.maximum(high, top[n, :, mine])
        if slot == 0:
            high = jnp.maximum(high, causal_stat[0])
        amount = jnp.zeros_like(high)
        pulled = jnp.zeros_like(high)
        for n in range(BLOCKS):
            part = total[n, :, mine] * jnp.exp2(top[n, :, mine] - high)
            amount += part
            pulled += part * mean[n, :, mine]
        if slot == 0:
            part = causal_stat[1] * jnp.exp2(causal_stat[0] - high)
            amount += part
            pulled += part * causal_stat[2]
        stat_own[slot, 0:1] = high
        stat_own[slot, 1:2] = amount
        stat_own[slot, 2:3] = pulled
        stat_own[slot, 3:8] = jnp.zeros((5, rows), F32)
    stats = [
        remote(stat_own.at[slot], stat_in.at[1 - slot], stat_send.at[slot], stat_recv.at[1 - slot], sibling)
        for slot in range(2)
    ]
    for copy in stats:
        copy.start()
    for copy in stats:
        copy.wait()
    for slot in range(2):
        mine = pl.ds(slot * rows, rows)
        high = jnp.maximum(stat_own[slot, 0:1], stat_in[slot, 0:1])
        left = jnp.exp2(stat_own[slot, 0:1] - high)
        right = jnp.exp2(stat_in[slot, 0:1] - high)
        amount = stat_own[slot, 1:2] * left + stat_in[slot, 1:2] * right
        log_total[:, mine] = high + jnp.log2(amount)
        delta[:, mine] = (stat_own[slot, 2:3] * left + stat_in[slot, 2:3] * right) / amount

    def second_pass(weights, pulled, high, centre, mine):
        attend = weights.astype(F32) * jnp.exp2(high - log_total[:, mine])
        slope = attend * (pulled.astype(F32) + (centre - delta[:, mine]))
        return attend.astype(BF16), slope.astype(BF16)

    for copy in shares:
        copy.wait_send()

    def to_owner(n, back, device):
        here = block(n)
        return [
            remote(k_all.at[here, :], dk_in.at[back], dk_send.at[n], dk_recv.at[back], device),
            remote(v_all.at[here, :], dv_in.at[back], dv_send.at[n], dv_recv.at[back], device),
        ]

    q_flat = q_all[...].reshape(2 * rows, q_all.shape[2])
    g_flat = g_all[...].reshape(2 * rows, q_all.shape[2])

    def gradient_block(n):
        here = block(n)
        parts = []
        for slot in range(2):
            mine = pl.ds(slot * rows, rows)
            attend, slope = second_pass(prob[here, mine], grad[here, mine], top[n, :, mine], mean[n, :, mine], mine)
            grad[here, mine] = slope
            parts.append((attend, slope))
        attend = jnp.concatenate([parts[0][0], parts[1][0]], axis=1)
        slope = jnp.concatenate([parts[0][1], parts[1][1]], axis=1)
        dv = jnp.dot(attend, g_flat, preferred_element_type=F32)
        dk = jnp.dot(slope, q_flat, preferred_element_type=F32) * scaling
        return dk, dv

    def gradient_step(u, carry):
        n = (u + 1) % BLOCKS
        here = block(n)
        dk, dv = gradient_block(n)

        @pl.when(n > 0)
        def _():
            k_all[here, :] = dk.astype(BF16)
            v_all[here, :] = dv.astype(BF16)

        @pl.when(n == 0)
        def _():
            own[0] = dk
            own[1] = dv

        for place in range(1, BLOCKS):

            @pl.when(n == place)
            def _():
                for copy in to_owner(place, BACK[place], class_mate(place)):
                    copy.start()

        return carry

    lax.fori_loop(0, BLOCKS, gradient_step, 0)

    columns = 256

    def turned_slot(slot):
        def part(i, carry):
            there = pl.ds(pl.multiple_of(slot * rows + i * columns, columns), columns)
            dq_turned[:, there] = jnp.dot(k_turned[...], grad[:, there], preferred_element_type=F32)
            return carry

        lax.fori_loop(0, rows // columns, part, 0)

    turned_slot(1)
    give_dq = remote(dq_turned.at[:, pl.ds(rows, rows)], dq_in, dq_send.at[0], dq_recv.at[0], sibling)
    give_dq.start()
    turned_slot(0)
    mine = pl.ds(0, rows)
    attend, slope = second_pass(causal_p[...], causal_d[...], causal_stat[0], causal_stat[2], mine)
    wide = q_all.shape[2]
    flat[:, group * wide : (group + 1) * wide] = (
        jnp.dot(slope, q_all[0], preferred_element_type=F32) * scaling
    ).astype(BF16)
    flat[:, (group + 1) * wide :] = jnp.dot(attend, g_all[0], preferred_element_type=F32).astype(BF16)
    self_part = jnp.dot(rk[...].T, slope, preferred_element_type=F32)
    give_dq.wait_recv()
    dq_rows[...] = ((dq_turned[:, mine] + self_part + dq_in[...]) * scaling).T
    for i in range(group):
        flat[:, i * wide : (i + 1) * wide] = dq_rows[pl.ds(i, self_rows, stride=group), :].astype(BF16)

    share_rows = hidden_out.shape[0]

    def hidden_copy(c, e):
        there = head_index(e)
        back = (e // 4) * 4 + (4 - e % 4) % 4
        piece = pl.ds(pl.multiple_of(c * CHUNK, CHUNK), CHUNK)
        return remote(
            hid.at[pl.ds(pl.multiple_of(there * share_rows, share_rows), share_rows), piece],
            hid_in.at[back, :, piece],
            hid_send.at[c, e],
            hid_recv.at[c, back],
            (there, resp),
        )

    def hidden_chunk(c, carry):
        slot = c % SLOTS
        for load in weight_loads(c, slot):
            load.wait()
        turned = lax.dot_general(weight[slot], flat[...], NT, preferred_element_type=F32)
        piece = pl.ds(pl.multiple_of(c * CHUNK, CHUNK), CHUNK)
        hid[:, piece] = turned.T.astype(BF16)
        for e in range(1, 8):
            hidden_copy(c, e).start()

        @pl.when(c + SLOTS < chunks)
        def _():
            for load in weight_loads(c + SLOTS, slot):
                load.start()

        return carry

    lax.fori_loop(0, chunks, hidden_chunk, 0)

    dk, dv = own[0], own[1]
    for n in range(1, BLOCKS):
        back = BACK[n]
        for copy in to_owner(back, n, class_mate(back)):
            copy.wait_recv()
        dk = dk + dk_in[n].astype(F32)
        dv = dv + dv_in[n].astype(F32)
    dk_out[...] = dk.astype(BF16)
    dv_out[...] = dv.astype(BF16)

    def hidden_wait(c, carry):
        for e in range(1, 8):
            hidden_copy(c, e).wait()
        return carry

    lax.fori_loop(0, chunks, hidden_wait, 0)
    result = hid[pl.ds(pl.multiple_of(head * share_rows, share_rows), share_rows), :].astype(F32)
    for e in range(1, 8):
        result = result + hid_in[e].astype(F32)
    hidden_out[...] = result.astype(BF16)

    for n in range(1, BLOCKS):
        for copy in to_owner(n, BACK[n], class_mate(n)):
            copy.wait_send()
    for copy in pair + [give_dq]:
        copy.wait_send()


def per_device(
    queries, resp_keys, resp_values, out_grad, prefix_keys, prefix_values, w_query, w_key, w_value, resp_lengths
):
    self_rows, group, size = queries.shape[1:]
    rows = self_rows * group
    width = w_query.shape[0]
    heads = 8
    keys = BLOCKS * SHARE
    chunks = width // CHUNK
    vmem, dma = pltpu.VMEM, pltpu.SemaphoreType.DMA
    whole = pl.BlockSpec(memory_space=pltpu.VMEM)
    hidden, dk, dv = pl.pallas_call(
        kernel,
        out_shape=(
            jax.ShapeDtypeStruct((self_rows // heads, width), BF16),
            jax.ShapeDtypeStruct((SHARE, size), BF16),
            jax.ShapeDtypeStruct((SHARE, size), BF16),
        ),
        in_specs=[pl.BlockSpec(memory_space=pltpu.SMEM)] + [pl.BlockSpec(memory_space=pl.ANY)] * 9,
        out_specs=(whole, whole, whole),
        scratch_shapes=[
            vmem((2, rows, size), BF16),
            vmem((2, rows, size), BF16),
            vmem((keys, size), BF16),
            vmem((keys, size), BF16),
            vmem((2, rows, 2 * size), BF16),
            vmem((size, keys), BF16),
            vmem((keys, 2 * rows), BF16),
            vmem((keys, 2 * rows), BF16),
            vmem((BLOCKS, 1, 2 * rows), F32),
            vmem((BLOCKS, 1, 2 * rows), F32),
            vmem((BLOCKS, 1, 2 * rows), F32),
            vmem((1, 2 * rows), F32),
            vmem((1, 2 * rows), F32),
            vmem((self_rows, size), BF16),
            vmem((self_rows, size), BF16),
            vmem((self_rows, rows), BF16),
            vmem((self_rows, rows), BF16),
            vmem((3, 1, rows), F32),
            vmem((2, 8, rows), F32),
            vmem((2, 8, rows), F32),
            vmem((size, 2 * rows), F32),
            vmem((size, rows), F32),
            vmem((rows, size), F32),
            vmem((self_rows, (group + 2) * size), BF16),
            vmem((SLOTS, CHUNK, (group + 2) * size), BF16),
            vmem((self_rows, width), BF16),
            vmem((heads, self_rows // heads, width), BF16),
            vmem((2, SHARE, size), F32),
            vmem((BLOCKS, SHARE, size), BF16),
            vmem((BLOCKS, SHARE, size), BF16),
            dma((6,)),
            dma((SLOTS, 3)),
            dma((2,)),
            dma((2,)),
            dma((BLOCKS,)),
            dma((BLOCKS,)),
            dma((BLOCKS,)),
            dma((BLOCKS,)),
            dma((2,)),
            dma((2,)),
            dma((1,)),
            dma((1,)),
            dma((BLOCKS,)),
            dma((BLOCKS,)),
            dma((BLOCKS,)),
            dma((BLOCKS,)),
            dma((chunks, 8)),
            dma((chunks, 8)),
        ],
        compiler_params=pltpu.CompilerParams(
            collective_id=0, has_side_effects=True, vmem_limit_bytes=63 * 1024 * 1024
        ),
    )(
        resp_lengths,
        queries.reshape(rows, size),
        out_grad.reshape(rows, size),
        resp_keys.reshape(self_rows, size),
        resp_values.reshape(self_rows, size),
        prefix_keys.reshape(SHARE, size),
        prefix_values.reshape(SHARE, size),
        w_query,
        w_key,
        w_value,
    )
    return hidden[None], dk[:, None], dv[:, None]


def solution(mesh):
    in_specs = (
        P("resp", None, "head", None),
        P("resp", None, "head", None),
        P("resp", None, "head", None),
        P("resp", None, "head", None),
        P("resp", "head", None),
        P("resp", "head", None),
        P(None, "head"),
        P(None, "head"),
        P(None, "head"),
        P(),
    )
    out_specs = (P("resp", "head", None), P("resp", "head", None), P("resp", "head", None))
    return jax.shard_map(
        per_device, mesh=mesh, in_specs=in_specs, out_specs=out_specs, check_vma=False
    )
```

time: 521 us -> 95.4 us (0.18)
  waiting for transfers between devices: 249 us -> 0 us
  matrix products: 218 us -> 0 us
  Pallas kernels: 0 us -> 89.9 us
  local copies, waits for them, and re-layouts: 20.9 us -> 4.73 us
  between operations: 13.9 us -> 0.64 us
  other arithmetic: 13.1 us -> 0 us
    dot_general x134 -> x0, matrix products: 218 us -> none  [the longest x49 74.4 us: logits(): jnp.einsum('rcgd,kcd->cgrk', query_part, key_tile, preferred_element_type...]
    reduce_scatter x3 -> x0, waiting for transfers between devices: 184 us -> none  [the longest x1 77.2 us: per_device(): lax.psum_scatter(key_parts.reshape(gathered_keys.shape).astype(jnp.bfloat...]
    pallas_call x0 -> x1, Pallas kernels: none -> 89.9 us  [per_device(): pl.pallas_call(kernel, out_shape=(jax.ShapeDtypeStruct((self_rows // head...]
    all_gather x2 -> x0, waiting for transfers between devices: 62.5 us -> none  [the longest x1 44.6 us: per_device(): lax.all_gather(prefix_keys, 'resp', axis=0, tiled=True)]
    while x144 -> x0, local copies, waits for them, and re-layouts: 17.1 us -> none
    reduce_sum x17 -> x0, other arithmetic: 6.97 us -> none  [running_total(): jnp.sum(jnp.exp(scores - new_high[..., None]), -1)]
  transfers between devices with their start and end apart: 5 -> 0, of which waited for: 5 -> 0; matrix products, arithmetic and copies ran while one was open for 8% -> 0% of each run, Pallas kernels for 0% -> 0%
where the time goes in v1:
time: 95.4 us; the launch traced here: 95.2 us
  Pallas kernels  89.9 us (94%)
  local copies, waits for them, and re-layouts  4.73 us (5%)
    pallas_call x1, Pallas kernels, per_device(): pl.pallas_call(kernel, out_shape=(jax.ShapeDtypeStruct((self_rows // head...  89.9 us
    unnamed x3, local copies, waits for them, and re-layouts  4.73 us

profile of v1, /device:TPU:1, one launch (start us, length us, event | category | flops | bytes accessed | tf_op | source)
XLA Modules:
  0.0 95.2 jit_solution(11050324797091505990)
XLA Ops:
  0.6 89.9 %shard_map.121 = (bf16[16,5120]{1,0:T(8,128)(2,1)}, bf16[512,128]{1,0:T(8,128)(2,1)}, bf16[512,128]{1,0:T(8,128)(2,1)}) custom-call(s32[16]{0:T(128)} %lengths.1, bf16[1024,128]{1,0:T(8,128)(2,1)} %bitcast.9, bf16[1024,128]{1,0:T(8,128)(2,1)} %bitcast.10, bf16[128,128]{1,0:T(8,128)(2,1)} %bitcast.16, bf16[128,128]{1,0:T(8,128)(2,1)} %bitcast.17, ...), custom_call_target="tpu_custom_call" | custom-call | tf_op jit(solution)/shard_map/pallas_call | solution.py:359
  90.5 1.6 %copy.16 = bf16[1,16,5120]{2,1,0:T(8,128)(2,1)} copy(bf16[1,16,5120]{2,1,0:T(8,128)(2,1)} %bitcast.11) | data formatting | bytes 327680
  92.1 1.6 %copy.17 = bf16[512,1,128]{2,0,1:T(8,128)(2,1)} copy(bf16[512,1,128]{2,0,1:T(8,128)(2,1)} %bitcast.15) | data formatting | bytes 262144
  93.7 1.6 %copy.18 = bf16[512,1,128]{2,0,1:T(8,128)(2,1)} copy(bf16[512,1,128]{2,0,1:T(8,128)(2,1)} %bitcast.14) | data formatting | bytes 262144

commit v2 on v1

v2 whole, which is shorter than its diff:
```python
import math

import jax
import jax.numpy as jnp
from jax import lax
from jax.experimental import pallas as pl
from jax.experimental.pallas import tpu as pltpu
from jax.sharding import PartitionSpec as P

MESH = pl.DeviceIdType.MESH
NT = (((1,), (1,)), ((), ()))
F32, BF16 = jnp.float32, jnp.bfloat16
PLACES = (0, 1, 3, 2)
BACK = (0, 2, 1, 3)
BLOCKS = 4
RESPS = 4
SHARE = 512
CHUNK = 512
SLOTS = 4


def kernel(
    lengths, q_hbm, g_hbm, rk_hbm, rv_hbm, k_hbm, v_hbm, wq_hbm, wk_hbm, wv_hbm,
    hidden_out, dk_out, dv_out,
    q_all, g_all, k_all, v_all, q_scaled, k_turned, prob, grad, top, total, mean,
    log_total, delta, rk, rv, causal_p, causal_d, causal_stat, stat_own, stat_in,
    dq_own, dq_give, dq_in, dq_far, dq_far_in, dq_rows, flat, weight, hid, hid_in, dk_sum, dv_sum, dk_in, dv_in,
    local_sem, weight_sem, q_send, q_recv, far_send, far_recv, relay_send, relay_recv, k_send, k_recv, v_send, v_recv,
    stat_send, stat_recv, dq_send, dq_recv, dk_send, dk_recv, dv_send, dv_recv, hid_send, hid_recv,
):
    rows, wide = q_all.shape[1:]
    self_rows = rk.shape[0]
    group = rows // self_rows
    half = rows // 2
    head = lax.axis_index("head")
    resp = lax.axis_index("resp")
    z_lo, y = head // 4, head % 4
    z_hi, x, core = resp // 8, (resp // 2) % 4, resp % 2
    scaling = wide ** -0.5
    log2e = math.log2(math.e)
    chunks = hid.shape[1] // CHUNK

    def along_x(n):
        return (head, z_hi * 8 + ((x + PLACES[n]) % 4) * 2 + core)

    def holder(slot):
        z_there = (z_hi + slot // 2) % 2
        core_there = (core + slot % 2) % 2
        return (head, z_there * 8 + x * 2 + core_there)

    def head_index(e):
        return ((z_lo + e // 4) % 2) * 4 + (y + e % 4) % 4

    loads = [
        pltpu.make_async_copy(source, target, local_sem.at[i])
        for i, (source, target) in enumerate(
            (
                (k_hbm, k_all.at[pl.ds(0, SHARE), :]),
                (v_hbm, v_all.at[pl.ds(0, SHARE), :]),
                (q_hbm, q_all.at[0]),
                (g_hbm, g_all.at[0]),
                (rk_hbm, rk),
                (rv_hbm, rv),
            )
        )
    ]
    for load in loads:
        load.start()

    def weight_loads(c, slot):
        piece = pl.ds(pl.multiple_of(c * CHUNK, CHUNK), CHUNK)
        width = group * wide
        return [
            pltpu.make_async_copy(wq_hbm.at[piece, :], weight.at[slot, :, pl.ds(0, width)], weight_sem.at[slot, 0]),
            pltpu.make_async_copy(wk_hbm.at[piece, :], weight.at[slot, :, pl.ds(width, wide)], weight_sem.at[slot, 1]),
            pltpu.make_async_copy(
                wv_hbm.at[piece, :], weight.at[slot, :, pl.ds(width + wide, wide)], weight_sem.at[slot, 2]
            ),
        ]

    barrier = pltpu.get_barrier_semaphore()
    partners = [along_x(n) for n in range(1, BLOCKS)] + [holder(s) for s in range(1, RESPS)]
    partners += [(head_index(e), resp) for e in range(1, 8)]
    for partner in partners:
        pl.semaphore_signal(barrier, inc=1, device_id=partner, device_id_type=MESH)

    for load in loads:
        load.wait()
    place = lax.broadcasted_iota(jnp.int32, (rows, 1), 0)
    live = place < lengths[resp] * group
    g_all[0] = jnp.where(live, g_all[0], jnp.zeros_like(g_all[0]))

    pl.semaphore_wait(barrier, len(partners))

    def remote(source, target, send, recv, device):
        return pltpu.make_async_remote_copy(
            src_ref=source, dst_ref=target, send_sem=send, recv_sem=recv, device_id=device, device_id_type=MESH
        )

    def block(n):
        return pl.ds(pl.multiple_of(n * SHARE, SHARE), SHARE)

    def halves(part, origin, target, send, recv, device):
        piece = pl.ds(part * half, half)
        return [
            remote(q_all.at[origin, piece, :], q_all.at[target, piece, :], send.at[part, 0], recv.at[part, 0], device),
            remote(g_all.at[origin, piece, :], g_all.at[target, piece, :], send.at[part, 1], recv.at[part, 1], device),
        ]

    far = [halves(part, 0, 2, far_send, far_recv, holder(2)) for part in range(2)]
    for copy in far[0]:
        copy.start()
    pair = [
        remote(q_all.at[0], q_all.at[1], q_send.at[0], q_recv.at[0], holder(1)),
        remote(g_all.at[0], g_all.at[1], q_send.at[1], q_recv.at[1], holder(1)),
    ]
    for copy in pair:
        copy.start()
    shares = []
    for n in range(1, BLOCKS):
        there, here = pl.ds(BACK[n] * SHARE, SHARE), pl.ds(0, SHARE)
        for held, send, recv in ((k_all, k_send, k_recv), (v_all, v_send, v_recv)):
            copy = remote(held.at[here, :], held.at[there, :], send.at[n], recv.at[BACK[n]], along_x(n))
            copy.start()
            shares.append(copy)
    for copy in far[1]:
        copy.start()
    for c in range(SLOTS):
        for load in weight_loads(c, c):
            load.start()

    def scale_queries(slot, start, size):
        piece = pl.ds(start, size)
        exact = q_all[slot, piece, :].astype(F32) * (scaling * log2e)
        high = exact.astype(BF16)
        q_scaled[slot, piece, :wide] = high
        q_scaled[slot, piece, wide:] = (exact - high.astype(F32)).astype(BF16)

    def first_pass(keys, values, slot, start, size, allowed):
        piece = pl.ds(start, size)
        twice = jnp.concatenate([keys, keys], axis=1)
        scores = lax.dot_general(twice, q_scaled[slot, piece, :], NT, preferred_element_type=F32)
        if allowed is not None:
            scores = jnp.where(allowed, scores, -1e30)
        pulled = lax.dot_general(values, g_all[slot, piece, :], NT, preferred_element_type=F32)
        high = jnp.max(scores, axis=0, keepdims=True)
        weights = jnp.exp2(scores - high)
        amount = jnp.sum(weights, axis=0, keepdims=True)
        centre = jnp.sum(weights * pulled, axis=0, keepdims=True) / amount
        return weights.astype(BF16), (pulled - centre).astype(BF16), high, amount, centre

    def score_block(n, parts):
        here = block(n)
        keys, values = k_all[here, :], v_all[here, :]
        for slot, start, size in parts:
            mine = pl.ds(slot * rows + start, size)
            prob[here, mine], grad[here, mine], high, amount, centre = first_pass(keys, values, slot, start, size, None)
            top[n, :, mine] = high
            total[n, :, mine] = amount
            mean[n, :, mine] = centre

    def take_share(n):
        here = block(n)
        for held, send, recv in ((k_all, k_send, k_recv), (v_all, v_send, v_recv)):
            remote(held.at[here, :], held.at[here, :], send.at[n], recv.at[n], holder(1)).wait_recv()

    def turn_keys(n):
        here = block(n)
        k_turned[:, here] = k_all[here, :].T

    relays = [halves(part, 2, 3, relay_send, relay_recv, holder(1)) for part in range(2)]

    def pass_on(part):
        for copy in far[part]:
            copy.wait_recv()
        for copy in relays[part]:
            copy.start()

    def take_relay(part):
        scale_queries(2, part * half, half)
        for copy in relays[part]:
            copy.wait_recv()
        scale_queries(3, part * half, half)

    near = ((0, 0, rows), (1, 0, rows))

    scale_queries(0, 0, rows)
    key_place = lax.broadcasted_iota(jnp.int32, (self_rows, rows), 0)
    row_place = lax.broadcasted_iota(jnp.int32, (self_rows, rows), 1) // group
    causal_p[...], causal_d[...], high, amount, centre = first_pass(
        rk[...], rv[...], 0, 0, rows, key_place <= row_place
    )
    causal_stat[0], causal_stat[1], causal_stat[2] = high, amount, centre
    for copy in pair:
        copy.wait_recv()
    scale_queries(1, 0, rows)

    def near_step(n, carry):
        @pl.when(n > 0)
        def _():
            take_share(n)

        @pl.when(n == 2)
        def _():
            pass_on(0)

        turn_keys(n)
        score_block(n, near)
        return carry

    lax.fori_loop(0, BLOCKS - 1, near_step, 0)
    take_relay(0)

    def far_step(part):
        def step(n, carry):
            score_block(n, ((2, part * half, half), (3, part * half, half)))
            return carry

        return step

    lax.fori_loop(0, BLOCKS - 1, far_step(0), 0)
    take_share(BLOCKS - 1)
    pass_on(1)
    turn_keys(BLOCKS - 1)
    score_block(BLOCKS - 1, near)
    far_step(0)(BLOCKS - 1, 0)
    take_relay(1)
    lax.fori_loop(0, BLOCKS, far_step(1), 0)

    for slot in range(RESPS):
        mine = pl.ds(slot * rows, rows)
        high = top[0, :, mine]
        for n in range(1, BLOCKS):
            high = jnp.maximum(high, top[n, :, mine])
        if slot == 0:
            high = jnp.maximum(high, causal_stat[0])
        amount = jnp.zeros_like(high)
        pulled = jnp.zeros_like(high)
        for n in range(BLOCKS):
            part = total[n, :, mine] * jnp.exp2(top[n, :, mine] - high)
            amount += part
            pulled += part * mean[n, :, mine]
        if slot == 0:
            part = causal_stat[1] * jnp.exp2(causal_stat[0] - high)
            amount += part
            pulled += part * causal_stat[2]
        stat_own[slot : slot + 1] = high + jnp.log2(amount)
        stat_own[RESPS + slot : RESPS + slot + 1] = pulled / amount
    stats = [
        remote(stat_own, stat_in.at[s], stat_send.at[s], stat_recv.at[s], holder(s)) for s in range(1, RESPS)
    ]
    for copy in stats:
        copy.start()
    dk_sum[...] = jnp.zeros_like(dk_sum)
    dv_sum[...] = jnp.zeros_like(dv_sum)
    for copy in stats:
        copy.wait()
    for slot in range(RESPS):
        mine = pl.ds(slot * rows, rows)
        logs = [stat_own[slot : slot + 1]]
        means = [stat_own[RESPS + slot : RESPS + slot + 1]]
        for s in range(1, RESPS):
            there = slot ^ s
            logs.append(stat_in[s, there : there + 1])
            means.append(stat_in[s, RESPS + there : RESPS + there + 1])
        high = jnp.maximum(jnp.maximum(logs[0], logs[1]), jnp.maximum(logs[2], logs[3]))
        parts = [jnp.exp2(value - high) for value in logs]
        amount = parts[0] + parts[1] + parts[2] + parts[3]
        pulled = parts[0] * means[0] + parts[1] * means[1] + parts[2] * means[2] + parts[3] * means[3]
        log_total[:, mine] = high + jnp.log2(amount)
        delta[:, mine] = pulled / amount

    def second_pass(weights, pulled, high, centre, mine):
        attend = weights.astype(F32) * jnp.exp2(high - log_total[:, mine])
        slope = attend * (pulled.astype(F32) + (centre - delta[:, mine]))
        return attend.astype(BF16), slope.astype(BF16)

    def gradient_slot(slot):
        mine = pl.ds(slot * rows, rows)
        for n in range(BLOCKS):
            here = pl.ds(n * SHARE, SHARE)
            attend, slope = second_pass(prob[here, mine], grad[here, mine], top[n, :, mine], mean[n, :, mine], mine)
            prob[here, mine] = attend
            grad[here, mine] = slope
        dv_sum[...] += jnp.dot(prob[:, mine], g_all[slot], preferred_element_type=F32)
        dk_sum[...] += jnp.dot(grad[:, mine], q_all[slot], preferred_element_type=F32)
        return jnp.dot(k_turned[...], grad[:, mine], preferred_element_type=F32)

    dq_give[0] = gradient_slot(3)
    give_far = remote(dq_give.at[0], dq_in.at[0], dq_send.at[0], dq_recv.at[0], holder(1))
    give_far.start()
    far_part = gradient_slot(2)
    give_far.wait_recv()
    dq_far[...] = (far_part + dq_in[0]).astype(BF16)
    give_back = remote(dq_far, dq_far_in, dq_send.at[2], dq_recv.at[2], holder(2))
    give_back.start()
    dq_give[1] = gradient_slot(1)
    give_near = remote(dq_give.at[1], dq_in.at[1], dq_send.at[1], dq_recv.at[1], holder(1))
    give_near.start()

    attend, slope = second_pass(
        causal_p[...], causal_d[...], causal_stat[0], causal_stat[2], pl.ds(0, rows)
    )
    flat[:, group * wide : (group + 1) * wide] = (
        jnp.dot(slope, q_all[0], preferred_element_type=F32) * scaling
    ).astype(BF16)
    flat[:, (group + 1) * wide :] = jnp.dot(attend, g_all[0], preferred_element_type=F32).astype(BF16)
    dq_own[...] = jnp.dot(rk[...].T, slope, preferred_element_type=F32)
    dq_own[...] += gradient_slot(0)

    for copy in shares:
        copy.wait_send()
    k_all[...] = (dk_sum[...] * scaling).astype(BF16)
    v_all[...] = dv_sum[...].astype(BF16)

    def to_owner(n):
        back, here, device = BACK[n], pl.ds(n * SHARE, SHARE), along_x(n)
        return [
            remote(k_all.at[here, :], dk_in.at[back], dk_send.at[n], dk_recv.at[back], device),
            remote(v_all.at[here, :], dv_in.at[back], dv_send.at[n], dv_recv.at[back], device),
        ]

    owed = [copy for n in range(1, BLOCKS) for copy in to_owner(n)]
    for copy in owed:
        copy.start()

    give_near.wait_recv()
    give_back.wait_recv()
    dq_rows[...] = ((dq_own[...] + dq_in[1] + dq_far_in[...].astype(F32)) * scaling).T
    for i in range(group):
        flat[:, i * wide : (i + 1) * wide] = dq_rows[pl.ds(i, self_rows, stride=group), :].astype(BF16)

    share_rows = hidden_out.shape[0]

    def hidden_copy(c, e):
        there = head_index(e)
        back = (e // 4) * 4 + (4 - e % 4) % 4
        piece = pl.ds(pl.multiple_of(c * CHUNK, CHUNK), CHUNK)
        return remote(
            hid.at[pl.ds(pl.multiple_of(there * share_rows, share_rows), share_rows), piece],
            hid_in.at[back, :, piece],
            hid_send.at[c, e],
            hid_recv.at[c, back],
            (there, resp),
        )

    def hidden_chunk(c, carry):
        slot = c % SLOTS
        for load in weight_loads(c, slot):
            load.wait()
        turned = lax.dot_general(weight[slot], flat[...], NT, preferred_element_type=F32)
        piece = pl.ds(pl.multiple_of(c * CHUNK, CHUNK), CHUNK)
        hid[:, piece] = turned.T.astype(BF16)
        for e in range(1, 8):
            hidden_copy(c, e).start()

        @pl.when(c + SLOTS < chunks)
        def _():
            for load in weight_loads(c + SLOTS, slot):
                load.start()

        return carry

    lax.fori_loop(0, chunks, hidden_chunk, 0)

    for copy in owed:
        copy.wait_recv()
    dk = dk_sum[pl.ds(0, SHARE), :] * scaling
    dv = dv_sum[pl.ds(0, SHARE), :]
    for n in range(1, BLOCKS):
        dk = dk + dk_in[n].astype(F32)
        dv = dv + dv_in[n].astype(F32)
    dk_out[...] = dk.astype(BF16)
    dv_out[...] = dv.astype(BF16)

    def hidden_wait(c, carry):
        for e in range(1, 8):
            hidden_copy(c, e).wait()
        return carry

    lax.fori_loop(0, chunks, hidden_wait, 0)
    result = hid[pl.ds(pl.multiple_of(head * share_rows, share_rows), share_rows), :].astype(F32)
    for e in range(1, 8):
        result = result + hid_in[e].astype(F32)
    hidden_out[...] = result.astype(BF16)

    for copy in pair + far[0] + far[1] + relays[0] + relays[1] + [give_far, give_near, give_back] + owed:
        copy.wait_send()


def per_device(
    queries, resp_keys, resp_values, out_grad, prefix_keys, prefix_values, w_query, w_key, w_value, resp_lengths
):
    self_rows, group, size = queries.shape[1:]
    rows = self_rows * group
    width = w_query.shape[0]
    heads = 8
    keys = BLOCKS * SHARE
    chunks = width // CHUNK
    vmem, dma = pltpu.VMEM, pltpu.SemaphoreType.DMA
    whole = pl.BlockSpec(memory_space=pltpu.VMEM)
    hidden, dk, dv = pl.pallas_call(
        kernel,
        out_shape=(
            jax.ShapeDtypeStruct((self_rows // heads, width), BF16),
            jax.ShapeDtypeStruct((SHARE, size), BF16),
            jax.ShapeDtypeStruct((SHARE, size), BF16),
        ),
        in_specs=[pl.BlockSpec(memory_space=pltpu.SMEM)] + [pl.BlockSpec(memory_space=pl.ANY)] * 9,
        out_specs=(whole, whole, whole),
        scratch_shapes=[
            vmem((RESPS, rows, size), BF16),
            vmem((RESPS, rows, size), BF16),
            vmem((keys, size), BF16),
            vmem((keys, size), BF16),
            vmem((RESPS, rows, 2 * size), BF16),
            vmem((size, keys), BF16),
            vmem((keys, RESPS * rows), BF16),
            vmem((keys, RESPS * rows), BF16),
            vmem((BLOCKS, 1, RESPS * rows), F32),
            vmem((BLOCKS, 1, RESPS * rows), F32),
            vmem((BLOCKS, 1, RESPS * rows), F32),
            vmem((1, RESPS * rows), F32),
            vmem((1, RESPS * rows), F32),
            vmem((self_rows, size), BF16),
            vmem((self_rows, size), BF16),
            vmem((self_rows, rows), BF16),
            vmem((self_rows, rows), BF16),
            vmem((3, 1, rows), F32),
            vmem((2 * RESPS, rows), F32),
            vmem((RESPS, 2 * RESPS, rows), F32),
            vmem((size, rows), F32),
            vmem((2, size, rows), F32),
            vmem((2, size, rows), F32),
            vmem((size, rows), BF16),
            vmem((size, rows), BF16),
            vmem((rows, size), F32),
            vmem((self_rows, (group + 2) * size), BF16),
            vmem((SLOTS, CHUNK, (group + 2) * size), BF16),
            vmem((self_rows, width), BF16),
            vmem((heads, self_rows // heads, width), BF16),
            vmem((keys, size), F32),
            vmem((keys, size), F32),
            vmem((BLOCKS, SHARE, size), BF16),
            vmem((BLOCKS, SHARE, size), BF16),
            dma((6,)),
            dma((SLOTS, 3)),
            dma((2,)),
            dma((2,)),
            dma((2, 2)),
            dma((2, 2)),
            dma((2, 2)),
            dma((2, 2)),
            dma((BLOCKS,)),
            dma((BLOCKS,)),
            dma((BLOCKS,)),
            dma((BLOCKS,)),
            dma((RESPS,)),
            dma((RESPS,)),
            dma((3,)),
            dma((3,)),
            dma((BLOCKS,)),
            dma((BLOCKS,)),
            dma((BLOCKS,)),
            dma((BLOCKS,)),
            dma((chunks, 8)),
            dma((chunks, 8)),
        ],
        compiler_params=pltpu.CompilerParams(
            collective_id=0, has_side_effects=True, vmem_limit_bytes=63 * 1024 * 1024
        ),
    )(
        resp_lengths,
        queries.reshape(rows, size),
        out_grad.reshape(rows, size),
        resp_keys.reshape(self_rows, size),
        resp_values.reshape(self_rows, size),
        prefix_keys.reshape(SHARE, size),
        prefix_values.reshape(SHARE, size),
        w_query,
        w_key,
        w_value,
    )
    return hidden[None], dk[:, None], dv[:, None]


def solution(mesh):
    in_specs = (
        P("resp", None, "head", None),
        P("resp", None, "head", None),
        P("resp", None, "head", None),
        P("resp", None, "head", None),
        P("resp", "head", None),
        P("resp", "head", None),
        P(None, "head"),
        P(None, "head"),
        P(None, "head"),
        P(),
    )
    out_specs = (P("resp", "head", None), P("resp", "head", None), P("resp", "head", None))
    return jax.shard_map(
        per_device, mesh=mesh, in_specs=in_specs, out_specs=out_specs, check_vma=False
    )
```

time: 95.4 us -> 75.4 us (0.79)
  Pallas kernels: 89.9 us -> 69.6 us
    pallas_call x1, Pallas kernels: 89.9 us -> 69.6 us  [per_device(): pl.pallas_call(kernel, out_shape=(jax.ShapeDtypeStruct((self_rows // head...]
where the time goes in v2:
time: 75.4 us; the launch traced here: 75 us
  Pallas kernels  69.6 us (92%)
  local copies, waits for them, and re-layouts  4.73 us (6%)
    pallas_call x1, Pallas kernels, per_device(): pl.pallas_call(kernel, out_shape=(jax.ShapeDtypeStruct((self_rows // head...  69.6 us
    unnamed x3, local copies, waits for them, and re-layouts  4.73 us

profile of v2, /device:TPU:1, one launch (start us, length us, event | category | flops | bytes accessed | tf_op | source)
XLA Modules:
  0.0 75.0 jit_solution(16448071050592714362)
XLA Ops:
  0.6 69.6 %shard_map.121 = (bf16[16,5120]{1,0:T(8,128)(2,1)}, bf16[512,128]{1,0:T(8,128)(2,1)}, bf16[512,128]{1,0:T(8,128)(2,1)}) custom-call(s32[16]{0:T(128)} %lengths.1, bf16[1024,128]{1,0:T(8,128)(2,1)} %bitcast.9, bf16[1024,128]{1,0:T(8,128)(2,1)} %bitcast.10, bf16[128,128]{1,0:T(8,128)(2,1)} %bitcast.16, bf16[128,128]{1,0:T(8,128)(2,1)} %bitcast.17, ...), custom_call_target="tpu_custom_call" | custom-call | tf_op jit(solution)/shard_map/pallas_call | solution.py:402
  70.2 1.6 %copy.16 = bf16[1,16,5120]{2,1,0:T(8,128)(2,1)} copy(bf16[1,16,5120]{2,1,0:T(8,128)(2,1)} %bitcast.11) | data formatting | bytes 327680
  71.8 1.6 %copy.17 = bf16[512,1,128]{2,0,1:T(8,128)(2,1)} copy(bf16[512,1,128]{2,0,1:T(8,128)(2,1)} %bitcast.15) | data formatting | bytes 262144
  73.4 1.6 %copy.18 = bf16[512,1,128]{2,0,1:T(8,128)(2,1)} copy(bf16[512,1,128]{2,0,1:T(8,128)(2,1)} %bitcast.14) | data formatting | bytes 262144

commit v3 on v2

v3 whole, which is shorter than its diff:
```python
import math

import jax
import jax.numpy as jnp
from jax import lax
from jax.experimental import pallas as pl
from jax.experimental.pallas import tpu as pltpu
from jax.sharding import PartitionSpec as P

MESH = pl.DeviceIdType.MESH
NT = (((1,), (1,)), ((), ()))
F32, BF16 = jnp.float32, jnp.bfloat16
PLACES = (0, 1, 3, 2)
BACK = (0, 2, 1, 3)
BLOCKS = 4
RESPS = 4
HEADS = 8
SHARE = 512
CHUNK = 512
RING = 4


def kernel(
    lengths, q_hbm, g_hbm, rk_hbm, rv_hbm, k_hbm, v_hbm, wq_hbm, wk_hbm, wv_hbm,
    hidden_out, dk_out, dv_out,
    q_all, g_all, k_all, v_all, q_scaled, k_turned, prob, grad, top, total, mean,
    log_total, delta, rk, rv, causal_p, causal_d, causal_stat, stat_own, stat_in,
    dq_self, dq_part, dq_in, dq_far, dq_far_in, dq_rows, self_flat, flat, weight, hid_in,
    dk_sum, dv_sum, dk_in, dv_in,
    local_sem, weight_sem, q_send, q_recv, far_send, far_recv, relay_send, relay_recv, k_send, k_recv, v_send, v_recv,
    stat_send, stat_recv, dq_send, dq_recv, dq_far_send, dq_far_recv, dk_send, dk_recv, dv_send, dv_recv,
    hid_send, hid_recv,
):
    pair_rows, wide = q_all.shape[2:]
    half = pair_rows // 2
    self_rows = rk.shape[0]
    group = 2 * half // self_rows
    head = lax.axis_index("head")
    resp = lax.axis_index("resp")
    z_lo, y = head // 4, head % 4
    z_hi, x, core = resp // 8, (resp // 2) % 4, resp % 2
    scaling = wide ** -0.5
    log2e = math.log2(math.e)
    steps = hid_in.shape[2]
    narrow = CHUNK // 2

    def along_x(n):
        return (head, z_hi * 8 + ((x + PLACES[n]) % 4) * 2 + core)

    def holder(slot):
        z_there = (z_hi + slot // 2) % 2
        core_there = (core + slot % 2) % 2
        return (head, z_there * 8 + x * 2 + core_there)

    def head_index(e):
        return ((z_lo + e // 4) % 2) * 4 + (y + e % 4) % 4

    def first(h, held):
        return held.at[h, 0, pl.ds(0, half), :]

    loads = [
        pltpu.make_async_copy(source, target, local_sem.at[i])
        for i, (source, target) in enumerate(
            (
                (k_hbm, k_all.at[pl.ds(0, SHARE), :]),
                (v_hbm, v_all.at[pl.ds(0, SHARE), :]),
                (rk_hbm, rk),
                (rv_hbm, rv),
            )
        )
    ]
    piece_rows = half // HEADS
    for h in range(2):
        for o in range(HEADS):
            for i, (source, held) in enumerate(((q_hbm, q_all), (g_hbm, g_all))):
                loads.append(
                    pltpu.make_async_copy(
                        source.at[pl.ds((2 * o + h) * piece_rows, piece_rows), :],
                        held.at[h, 0, pl.ds(o * piece_rows, piece_rows), :],
                        local_sem.at[4 + (h * HEADS + o) * 2 + i],
                    )
                )
    for load in loads:
        load.start()

    def weight_loads(v):
        slot, width = v % RING, group * wide
        piece = pl.ds(pl.multiple_of(((v // 2) % steps + (v % 2) * steps) * CHUNK, CHUNK), CHUNK)
        return [
            pltpu.make_async_copy(
                source.at[piece, :], weight.at[slot, :, pl.ds(start, size)], weight_sem.at[slot, j]
            )
            for j, (source, start, size) in enumerate(
                ((wq_hbm, 0, width), (wk_hbm, width, wide), (wv_hbm, width + wide, wide))
            )
        ]

    barrier = pltpu.get_barrier_semaphore()
    partners = [along_x(n) for n in range(1, BLOCKS)] + [holder(s) for s in range(1, RESPS)]
    partners += [(head_index(e), resp) for e in range(1, HEADS)]
    for partner in partners:
        pl.semaphore_signal(barrier, inc=1, device_id=partner, device_id_type=MESH)

    def row_of(h, count):
        return (count >> 6) * 16 + 8 * h + ((count & 63) >> 3)

    for load in loads:
        load.wait()
    for h in range(2):
        place = lax.broadcasted_iota(jnp.int32, (half, 1), 0)
        live = row_of(h, place) < lengths[resp]
        g_all[h, 0, :half] = jnp.where(live, g_all[h, 0, :half], jnp.zeros((half, wide), BF16))

    pl.semaphore_wait(barrier, len(partners))

    def remote(source, target, send, recv, device):
        return pltpu.make_async_remote_copy(
            src_ref=source, dst_ref=target, send_sem=send, recv_sem=recv, device_id=device, device_id_type=MESH
        )

    def block(n):
        return pl.ds(pl.multiple_of(n * SHARE, SHARE), SHARE)

    def rows_to(h, origin, target, send, recv, device):
        (pair, at), (pair_there, at_there) = origin, target
        return [
            remote(
                held.at[h, pair, pl.ds(at * half, half), :],
                held.at[h, pair_there, pl.ds(at_there * half, half), :],
                send.at[h, i],
                recv.at[h, i],
                device,
            )
            for i, held in enumerate((q_all, g_all))
        ]

    far = [rows_to(h, (0, 0), (1, 0), far_send, far_recv, holder(2)) for h in range(2)]
    near = [rows_to(h, (0, 0), (0, 1), q_send, q_recv, holder(1)) for h in range(2)]
    relays = [rows_to(h, (1, 0), (1, 1), relay_send, relay_recv, holder(1)) for h in range(2)]
    for copy in far[0] + near[0] + near[1]:
        copy.start()
    shares = []
    for n in range(1, BLOCKS):
        there, here = pl.ds(BACK[n] * SHARE, SHARE), pl.ds(0, SHARE)
        for held, send, recv in ((k_all, k_send, k_recv), (v_all, v_send, v_recv)):
            copy = remote(held.at[here, :], held.at[there, :], send.at[n], recv.at[BACK[n]], along_x(n))
            copy.start()
            shares.append(copy)
    for copy in far[1]:
        copy.start()
    for v in range(RING):
        for load in weight_loads(v):
            load.start()

    def scale_queries(h, pair, at):
        piece = pl.ds(at * half, half)
        exact = q_all[h, pair, piece, :].astype(F32) * (scaling * log2e)
        high = exact.astype(BF16)
        here = pl.ds((2 * h + pair) * pair_rows + at * half, half)
        q_scaled[here, :wide] = high
        q_scaled[here, wide:] = (exact - high.astype(F32)).astype(BF16)

    def first_pass(keys, values, scaled, pulls, allowed):
        twice = jnp.concatenate([keys, keys], axis=1)
        scores = lax.dot_general(twice, scaled, NT, preferred_element_type=F32)
        if allowed is not None:
            scores = jnp.where(allowed, scores, -1e30)
        pulled = lax.dot_general(values, pulls, NT, preferred_element_type=F32)
        high = jnp.max(scores, axis=0, keepdims=True)
        weights = jnp.exp2(scores - high)
        amount = jnp.sum(weights, axis=0, keepdims=True)
        centre = jnp.sum(weights * pulled, axis=0, keepdims=True) / amount
        return weights.astype(BF16), (pulled - centre).astype(BF16), high, amount, centre

    def pair_columns(h, pair):
        return pl.ds(pl.multiple_of((2 * h + pair) * pair_rows, pair_rows), pair_rows)

    def slot_columns(h, slot):
        return pl.ds((RESPS * h + slot) * half, half)

    def score(n, h, pair):
        here, mine = block(n), pair_columns(h, pair)
        prob[here, mine], grad[here, mine], high, amount, centre = first_pass(
            k_all[here, :], v_all[here, :], q_scaled[mine, :], g_all[h, pair], None
        )
        top[n, :, mine] = high
        total[n, :, mine] = amount
        mean[n, :, mine] = centre

    def take_share(n):
        here = block(n)
        for held, send, recv in ((k_all, k_send, k_recv), (v_all, v_send, v_recv)):
            remote(held.at[here, :], held.at[here, :], send.at[n], recv.at[n], holder(1)).wait_recv()

    def turn_keys(n):
        here = block(n)
        k_turned[:, here] = k_all[here, :].T

    def pass_on(h):
        for copy in far[h]:
            copy.wait_recv()
        for copy in relays[h]:
            copy.start()

    def take_relay(h):
        scale_queries(h, 1, 0)
        for copy in relays[h]:
            copy.wait_recv()
        scale_queries(h, 1, 1)

    for h in range(2):
        scale_queries(h, 0, 0)
        key_place = lax.broadcasted_iota(jnp.int32, (self_rows, half), 0)
        row_place = row_of(h, lax.broadcasted_iota(jnp.int32, (self_rows, half), 1))
        causal_p[h], causal_d[h], high, amount, centre = first_pass(
            rk[...], rv[...], q_scaled[pl.ds(2 * h * pair_rows, half), :], g_all[h, 0, :half], key_place <= row_place
        )
        causal_stat[h, 0], causal_stat[h, 1], causal_stat[h, 2] = high, amount, centre
    for copy in near[0] + near[1]:
        copy.wait_recv()
    scale_queries(0, 0, 1)
    scale_queries(1, 0, 1)

    def near_step(n, carry):
        @pl.when(n > 0)
        def _():
            take_share(n)

        @pl.when(n == 2)
        def _():
            pass_on(0)

        turn_keys(n)
        score(n, 0, 0)
        score(n, 1, 0)
        return carry

    def local_stats(h):
        for slot in range(RESPS):
            mine = slot_columns(h, slot)
            high = top[0, :, mine]
            for n in range(1, BLOCKS):
                high = jnp.maximum(high, top[n, :, mine])
            if slot == 0:
                high = jnp.maximum(high, causal_stat[h, 0])
            amount = jnp.zeros_like(high)
            pulled = jnp.zeros_like(high)
            for n in range(BLOCKS):
                part = total[n, :, mine] * jnp.exp2(top[n, :, mine] - high)
                amount += part
                pulled += part * mean[n, :, mine]
            if slot == 0:
                part = causal_stat[h, 1] * jnp.exp2(causal_stat[h, 0] - high)
                amount += part
                pulled += part * causal_stat[h, 2]
            stat_own[h, slot : slot + 1] = high + jnp.log2(amount)
            stat_own[h, RESPS + slot : RESPS + slot + 1] = pulled / amount

    stats = [
        [
            remote(stat_own.at[h], stat_in.at[h, s], stat_send.at[h, s], stat_recv.at[h, s], holder(s))
            for s in range(1, RESPS)
        ]
        for h in range(2)
    ]

    def all_stats(h):
        for copy in stats[h]:
            copy.wait_recv()
        for slot in range(RESPS):
            mine = slot_columns(h, slot)
            logs = [stat_own[h, slot : slot + 1]]
            means = [stat_own[h, RESPS + slot : RESPS + slot + 1]]
            for s in range(1, RESPS):
                there = slot ^ s
                logs.append(stat_in[h, s, there : there + 1])
                means.append(stat_in[h, s, RESPS + there : RESPS + there + 1])
            high = jnp.maximum(jnp.maximum(logs[0], logs[1]), jnp.maximum(logs[2], logs[3]))
            parts = [jnp.exp2(value - high) for value in logs]
            amount = parts[0] + parts[1] + parts[2] + parts[3]
            pulled = parts[0] * means[0] + parts[1] * means[1] + parts[2] * means[2] + parts[3] * means[3]
            log_total[:, mine] = high + jnp.log2(amount)
            delta[:, mine] = pulled / amount

    lax.fori_loop(0, BLOCKS - 1, near_step, 0)
    take_relay(0)
    for n in range(BLOCKS - 1):
        score(n, 0, 1)
    take_share(BLOCKS - 1)
    pass_on(1)
    turn_keys(BLOCKS - 1)
    score(BLOCKS - 1, 0, 0)
    score(BLOCKS - 1, 0, 1)
    local_stats(0)
    for copy in stats[0]:
        copy.start()
    score(BLOCKS - 1, 1, 0)
    take_relay(1)

    def far_step(i, carry):
        score(2 * i, 1, 1)
        score(2 * i + 1, 1, 1)
        return carry

    lax.fori_loop(0, BLOCKS // 2, far_step, 0)
    local_stats(1)
    for copy in stats[1]:
        copy.start()
    dk_sum[...] = jnp.zeros_like(dk_sum)
    dv_sum[...] = jnp.zeros_like(dv_sum)
    all_stats(0)

    def second_pass(weights, pulled, high, centre, mine):
        attend = weights.astype(F32) * jnp.exp2(high - log_total[:, mine])
        slope = attend * (pulled.astype(F32) + (centre - delta[:, mine]))
        return attend.astype(BF16), slope.astype(BF16)

    def causal_gradients():
        dk = jnp.zeros((self_rows, wide), F32)
        dv = jnp.zeros((self_rows, wide), F32)
        for h in range(2):
            attend, slope = second_pass(
                causal_p[h], causal_d[h], causal_stat[h, 0], causal_stat[h, 2], slot_columns(h, 0)
            )
            dk += jnp.dot(slope, q_all[h, 0, :half], preferred_element_type=F32)
            dv += jnp.dot(attend, g_all[h, 0, :half], preferred_element_type=F32)
            dq_self[h] = jnp.dot(rk[...].T, slope, preferred_element_type=F32)
        self_flat[:, :wide] = dk * scaling
        self_flat[:, wide:] = dv

    def give(u):
        return remote(
            dq_part.at[u % 2, :, pl.ds(half, half)], dq_in.at[u], dq_send.at[u], dq_recv.at[u], holder(1)
        )

    def give_far(h):
        return remote(dq_far.at[h], dq_far_in.at[h], dq_far_send.at[h], dq_far_recv.at[h], holder(2))

    def send_far(h):
        give(2 * h).wait_recv()
        dq_far[h] = (dq_part[0, :, :half] + dq_in[2 * h]).astype(BF16)
        give_far(h).start()

    def fill_flat(h):
        give(2 * h + 1).wait_recv()
        give_far(h).wait_recv()
        whole = dq_part[1, :, :half] + dq_self[h] + dq_in[2 * h + 1] + dq_far_in[h].astype(F32)
        dq_rows[...] = (whole * scaling).T
        for i in range(group):
            flat[h, :, i * wide : (i + 1) * wide] = dq_rows[
                pl.ds(i, self_rows // 2, stride=group), :
            ].astype(BF16)
        both = self_flat[...].reshape(HEADS, 2, 8, 2 * wide)[:, h].reshape(self_rows // 2, 2 * wide)
        flat[h, :, group * wide :] = both.astype(BF16)

    def hidden_piece(h, t, there):
        return q_scaled.at[pl.ds(pl.multiple_of(((h * steps + t) * HEADS + there) * 32, 32), 32), :]

    def group_columns(t, k):
        return pl.ds(pl.multiple_of((t + (k // 2) * steps) * CHUNK + (k % 2) * narrow, narrow), narrow)

    def hidden_copy(h, t, e):
        there = head_index(e)
        back = (e // 4) * 4 + (4 - e % 4) % 4
        return remote(
            hidden_piece(h, t, there),
            hid_in.at[back - 1, h, t],
            hid_send.at[h, t, e],
            hid_recv.at[h, t, back],
            (there, resp),
        )

    def project(h, start, stop):
        def step(t, carry):
            v = 2 * (h * steps + t)
            for i in range(2):
                for load in weight_loads(v + i):
                    load.wait()
            sides = []
            for i in range(2):
                turned = lax.dot_general(weight[(v + i) % RING], flat[h], NT, preferred_element_type=F32)
                for k in range(2):
                    part = turned[k * narrow : (k + 1) * narrow].T
                    sides.append(part.reshape(HEADS, 1, 8, narrow))
            here = pl.ds(pl.multiple_of((h * steps + t) * HEADS * 32, 32), HEADS * 32)
            q_scaled[here, :] = jnp.concatenate(sides, axis=1).reshape(HEADS * 32, narrow).astype(BF16)
            for e in range(1, HEADS):
                hidden_copy(h, t, e).start()

            @pl.when(v + RING < 4 * steps)
            def _():
                for i in range(2):
                    for load in weight_loads(v + RING + i):
                        load.start()

            return carry

        lax.fori_loop(start, stop, step, 0)

    def to_owner(n):
        back, here, device = BACK[n], pl.ds(n * SHARE, SHARE), along_x(n)
        return [
            remote(v_all.at[here, :], dv_in.at[back - 1], dv_send.at[n], dv_recv.at[back], device),
            remote(k_all.at[here, :], dk_in.at[back - 1], dk_send.at[n], dk_recv.at[back], device),
        ]

    owed = [copy for n in range(1, BLOCKS) for copy in to_owner(n)]

    def gradient_unit(u, carry):
        h, pair = u // 2, 1 - u % 2
        mine = pair_columns(h, pair)

        @pl.when(u > 1)
        def _():
            give(u - 2).wait_send()

        for n in range(BLOCKS):
            here = pl.ds(n * SHARE, SHARE)
            attend, slope = second_pass(prob[here, mine], grad[here, mine], top[n, :, mine], mean[n, :, mine], mine)
            prob[here, mine] = attend
            grad[here, mine] = slope
        dv_sum[...] += jnp.dot(prob[:, mine], g_all[h, pair], preferred_element_type=F32)
        dk_sum[...] += jnp.dot(grad[:, mine], q_all[h, pair], preferred_element_type=F32)
        dq_part[u % 2] = jnp.dot(k_turned[...], grad[:, mine], preferred_element_type=F32)
        give(u).start()

        @pl.when(u == 0)
        def _():
            all_stats(1)
            causal_gradients()
            send_far(0)

        @pl.when(u == 2)
        def _():
            fill_flat(0)
            send_far(1)

        return carry

    lax.fori_loop(0, 4, gradient_unit, 0)

    for copy in shares:
        copy.wait_send()
    v_all[...] = dv_sum[...].astype(BF16)
    k_all[...] = (dk_sum[...] * scaling).astype(BF16)
    for copy in owed:
        copy.start()
    project(0, 0, steps)
    fill_flat(1)
    project(1, 0, steps)

    for copy in owed:
        copy.wait_recv()
    dk = dk_sum[pl.ds(0, SHARE), :] * scaling
    dv = dv_sum[pl.ds(0, SHARE), :]
    for n in range(1, BLOCKS):
        dk = dk + dk_in[n - 1].astype(F32)
        dv = dv + dv_in[n - 1].astype(F32)
    dk_out[...] = dk.astype(BF16)
    dv_out[...] = dv.astype(BF16)

    def hidden_step(t, carry):
        sums = []
        for h in range(2):
            for e in range(1, HEADS):
                hidden_copy(h, t, e).wait()
            result = hidden_piece(h, t, head)[...].astype(F32)
            for e in range(1, HEADS):
                result = result + hid_in[e - 1, h, t].astype(F32)
            sums.append(result)
        for k in range(4):
            rows = [result[8 * k : 8 * k + 8] for result in sums]
            hidden_out[:, group_columns(t, k)] = jnp.concatenate(rows, axis=0).astype(BF16)
        return carry

    lax.fori_loop(0, steps, hidden_step, 0)

    sent = far[0] + far[1] + near[0] + near[1] + relays[0] + relays[1] + stats[0] + stats[1] + owed
    sent += [give(2), give(3)] + [give_far(0), give_far(1)]
    for copy in sent:
        copy.wait_send()


def finish_kernel(hidden_in, dk_in, dv_in, hidden_out, dk_out, dv_out):
    hidden_out[...] = hidden_in[...]
    dk_out[...] = dk_in[...]
    dv_out[...] = dv_in[...]


def per_device(
    queries, resp_keys, resp_values, out_grad, prefix_keys, prefix_values, w_query, w_key, w_value, resp_lengths
):
    self_rows, group, size = queries.shape[1:]
    rows = self_rows * group
    half = rows // 2
    width = w_query.shape[0]
    keys = BLOCKS * SHARE
    steps = width // CHUNK // 2
    vmem, dma = pltpu.VMEM, pltpu.SemaphoreType.DMA
    whole = pl.BlockSpec(memory_space=pltpu.VMEM)
    outputs = (
        jax.ShapeDtypeStruct((self_rows // HEADS, width), BF16),
        jax.ShapeDtypeStruct((SHARE, size), BF16),
        jax.ShapeDtypeStruct((SHARE, size), BF16),
    )
    results = pl.pallas_call(
        kernel,
        out_shape=outputs,
        in_specs=[pl.BlockSpec(memory_space=pltpu.SMEM)] + [pl.BlockSpec(memory_space=pl.ANY)] * 9,
        out_specs=(whole, whole, whole),
        scratch_shapes=[
            vmem((2, 2, rows, size), BF16),
            vmem((2, 2, rows, size), BF16),
            vmem((keys, size), BF16),
            vmem((keys, size), BF16),
            vmem((RESPS * rows, 2 * size), BF16),
            vmem((size, keys), BF16),
            vmem((keys, RESPS * rows), BF16),
            vmem((keys, RESPS * rows), BF16),
            vmem((BLOCKS, 1, RESPS * rows), F32),
            vmem((BLOCKS, 1, RESPS * rows), F32),
            vmem((BLOCKS, 1, RESPS * rows), F32),
            vmem((1, RESPS * rows), F32),
            vmem((1, RESPS * rows), F32),
            vmem((self_rows, size), BF16),
            vmem((self_rows, size), BF16),
            vmem((2, self_rows, half), BF16),
            vmem((2, self_rows, half), BF16),
            vmem((2, 3, 1, half), F32),
            vmem((2, 2 * RESPS, half), F32),
            vmem((2, RESPS, 2 * RESPS, half), F32),
            vmem((2, size, half), F32),
            vmem((2, size, rows), F32),
            vmem((4, size, half), F32),
            vmem((2, size, half), BF16),
            vmem((2, size, half), BF16),
            vmem((half, size), F32),
            vmem((self_rows, 2 * size), F32),
            vmem((2, self_rows // 2, (group + 2) * size), BF16),
            vmem((RING, CHUNK, (group + 2) * size), BF16),
            vmem((HEADS - 1, 2, steps, 2 * self_rows // HEADS, CHUNK // 2), BF16),
            vmem((keys, size), F32),
            vmem((keys, size), F32),
            vmem((BLOCKS - 1, SHARE, size), BF16),
            vmem((BLOCKS - 1, SHARE, size), BF16),
            dma((4 + 4 * HEADS,)),
            dma((RING, 3)),
            dma((2, 2)),
            dma((2, 2)),
            dma((2, 2)),
            dma((2, 2)),
            dma((2, 2)),
            dma((2, 2)),
            dma((BLOCKS,)),
            dma((BLOCKS,)),
            dma((BLOCKS,)),
            dma((BLOCKS,)),
            dma((2, RESPS)),
            dma((2, RESPS)),
            dma((4,)),
            dma((4,)),
            dma((2,)),
            dma((2,)),
            dma((BLOCKS,)),
            dma((BLOCKS,)),
            dma((BLOCKS,)),
            dma((BLOCKS,)),
            dma((2, steps, HEADS)),
            dma((2, steps, HEADS)),
        ],
        compiler_params=pltpu.CompilerParams(
            collective_id=0, has_side_effects=True, vmem_limit_bytes=65400 * 1024
        ),
    )(
        resp_lengths,
        queries.reshape(rows, size),
        out_grad.reshape(rows, size),
        resp_keys.reshape(self_rows, size),
        resp_values.reshape(self_rows, size),
        prefix_keys.reshape(SHARE, size),
        prefix_values.reshape(SHARE, size),
        w_query,
        w_key,
        w_value,
    )
    hidden, dk, dv = pl.pallas_call(
        finish_kernel, out_shape=outputs, in_specs=[whole] * 3, out_specs=(whole,) * 3
    )(*results)
    return hidden[None], dk[:, None], dv[:, None]


def solution(mesh):
    in_specs = (
        P("resp", None, "head", None),
        P("resp", None, "head", None),
        P("resp", None, "head", None),
        P("resp", None, "head", None),
        P("resp", "head", None),
        P("resp", "head", None),
        P(None, "head"),
        P(None, "head"),
        P(None, "head"),
        P(),
    )
    out_specs = (P("resp", "head", None), P("resp", "head", None), P("resp", "head", None))
    return jax.shard_map(
        per_device, mesh=mesh, in_specs=in_specs, out_specs=out_specs, check_vma=False
    )
```

time: 75.4 us -> 69.1 us (0.916)
  local copies, waits for them, and re-layouts: 4.73 us -> 0 us
  Pallas kernels: 69.6 us -> 68.1 us
    unnamed x3 -> x0, local copies, waits for them, and re-layouts: 4.73 us -> none
    pallas_call x1 -> x2, Pallas kernels: 69.6 us -> 68.1 us  [the longest x1 66.3 us: per_device(): pl.pallas_call(kernel, out_shape=outputs, in_specs=[pl.BlockSpec(memory_s...]
where the time goes in v3:
time: 69.1 us; the launch traced here: 68.8 us
  Pallas kernels  68.1 us (99%)
    pallas_call x1, Pallas kernels, per_device(): pl.pallas_call(kernel, out_shape=outputs, in_specs=[pl.BlockSpec(memory_s...  66.3 us
    pallas_call x1, Pallas kernels, per_device(): pl.pallas_call(finish_kernel, out_shape=outputs, in_specs=[whole] * 3, ou...  1.81 us

profile of v3, /device:TPU:1, one launch (start us, length us, event | category | flops | bytes accessed | tf_op | source)
XLA Modules:
  0.0 68.8 jit_solution(9402859978588845693)
XLA Ops:
  0.6 66.3 %shard_map.121 = (bf16[16,5120]{1,0:T(8,128)(2,1)}, bf16[512,128]{1,0:T(8,128)(2,1)}, bf16[512,128]{1,0:T(8,128)(2,1)}) custom-call(s32[16]{0:T(128)} %lengths.1, bf16[1024,128]{1,0:T(8,128)(2,1)} %bitcast.9, bf16[1024,128]{1,0:T(8,128)(2,1)} %bitcast.10, bf16[128,128]{1,0:T(8,128)(2,1)} %bitcast.13, bf16[128,128]{1,0:T(8,128)(2,1)} %bitcast.14, ...), custom_call_target="tpu_custom_call" | custom-call | tf_op jit(solution)/shard_map/pallas_call | solution.py:506
  67.0 1.8 %shard_map.122 = (bf16[16,5120]{1,0:T(8,128)(2,1)}, bf16[512,128]{1,0:T(8,128)(2,1)}, bf16[512,128]{1,0:T(8,128)(2,1)}) custom-call(bf16[16,5120]{1,0:T(8,128)(2,1)} %get-tuple-element.9.hidden_in, bf16[512,128]{1,0:T(8,128)(2,1)} %get-tuple-element.10.dk_in, bf16[512,128]{1,0:T(8,128)(2,1)} %get-tuple-element.11.dv_in), custom_call_target="tpu_custom_call" | custom-call | tf_op jit(solution)/shard_map/pallas_call | solution.py:586

commit v4 on v3

--- a/solution.py
+++ b/solution.py
@@ -21,9 +21,9 @@
 
 
 def kernel(
-    lengths, q_hbm, g_hbm, rk_hbm, rv_hbm, k_hbm, v_hbm, wq_hbm, wk_hbm, wv_hbm,
+    lengths_hbm, q_hbm, g_hbm, rk_hbm, rv_hbm, k_hbm, v_hbm, wq_hbm, wk_hbm, wv_hbm,
     hidden_out, dk_out, dv_out,
-    q_all, g_all, k_all, v_all, q_scaled, k_turned, prob, grad, top, total, mean,
+    lengths, q_all, g_all, k_all, v_all, q_scaled, k_turned, prob, grad, top, total, mean,
     log_total, delta, rk, rv, causal_p, causal_d, causal_stat, stat_own, stat_in,
     dq_self, dq_part, dq_in, dq_far, dq_far_in, dq_rows, self_flat, flat, weight, hid_in,
     dk_sum, dv_sum, dk_in, dv_in,
@@ -66,6 +66,7 @@
                 (v_hbm, v_all.at[pl.ds(0, SHARE), :]),
                 (rk_hbm, rk),
                 (rv_hbm, rv),
+                (lengths_hbm, lengths),
             )
         )
     ]
@@ -77,7 +78,7 @@
                     pltpu.make_async_copy(
                         source.at[pl.ds((2 * o + h) * piece_rows, piece_rows), :],
                         held.at[h, 0, pl.ds(o * piece_rows, piece_rows), :],
-                        local_sem.at[4 + (h * HEADS + o) * 2 + i],
+                        local_sem.at[5 + (h * HEADS + o) * 2 + i],
                     )
                 )
     for load in loads:
@@ -324,7 +325,8 @@
             )
             dk += jnp.dot(slope, q_all[h, 0, :half], preferred_element_type=F32)
             dv += jnp.dot(attend, g_all[h, 0, :half], preferred_element_type=F32)
-            dq_self[h] = jnp.dot(rk[...].T, slope, preferred_element_type=F32)
+            turned = jnp.dot(rk[...].T, slope, preferred_element_type=F32)
+            dq_self[h] = turned if h else dq_self[h] + turned
         self_flat[:, :wide] = dk * scaling
         self_flat[:, wide:] = dv
 
@@ -344,7 +346,9 @@
     def fill_flat(h):
         give(2 * h + 1).wait_recv()
         give_far(h).wait_recv()
-        whole = dq_part[1, :, :half] + dq_self[h] + dq_in[2 * h + 1] + dq_far_in[h].astype(F32)
+        whole = dq_self[h] + dq_in[2 * h + 1] + dq_far_in[h].astype(F32)
+        if h:
+            whole = whole + dq_part[1, :, :half]
         dq_rows[...] = (whole * scaling).T
         for i in range(group):
             flat[h, :, i * wide : (i + 1) * wide] = dq_rows[
@@ -414,25 +418,29 @@
         def _():
             give(u - 2).wait_send()
 
+        slopes = []
         for n in range(BLOCKS):
             here = pl.ds(n * SHARE, SHARE)
             attend, slope = second_pass(prob[here, mine], grad[here, mine], top[n, :, mine], mean[n, :, mine], mine)
-            prob[here, mine] = attend
-            grad[here, mine] = slope
-        dv_sum[...] += jnp.dot(prob[:, mine], g_all[h, pair], preferred_element_type=F32)
-        dk_sum[...] += jnp.dot(grad[:, mine], q_all[h, pair], preferred_element_type=F32)
-        dq_part[u % 2] = jnp.dot(k_turned[...], grad[:, mine], preferred_element_type=F32)
+            dv_sum[here, :] += jnp.dot(attend, g_all[h, pair], preferred_element_type=F32)
+            dk_sum[here, :] += jnp.dot(slope, q_all[h, pair], preferred_element_type=F32)
+            slopes.append(slope)
+        slopes = jnp.concatenate(slopes, axis=0)
+        dq_part[u % 2] = jnp.dot(k_turned[...], slopes, preferred_element_type=F32)
         give(u).start()
 
         @pl.when(u == 0)
         def _():
             all_stats(1)
-            causal_gradients()
+
+        @pl.when(u == 1)
+        def _():
+            dq_self[0] = dq_part[1, :, :half]
             send_far(0)
 
         @pl.when(u == 2)
         def _():
-            fill_flat(0)
+            causal_gradients()
             send_far(1)
 
         return carry
@@ -445,6 +453,7 @@
     k_all[...] = (dk_sum[...] * scaling).astype(BF16)
     for copy in owed:
         copy.start()
+    fill_flat(0)
     project(0, 0, steps)
     fill_flat(1)
     project(1, 0, steps)
@@ -506,9 +515,10 @@
     results = pl.pallas_call(
         kernel,
         out_shape=outputs,
-        in_specs=[pl.BlockSpec(memory_space=pltpu.SMEM)] + [pl.BlockSpec(memory_space=pl.ANY)] * 9,
+        in_specs=[pl.BlockSpec(memory_space=pl.ANY)] * 10,
         out_specs=(whole, whole, whole),
         scratch_shapes=[
+            pltpu.SMEM(resp_lengths.shape, jnp.int32),
             vmem((2, 2, rows, size), BF16),
             vmem((2, 2, rows, size), BF16),
             vmem((keys, size), BF16),
@@ -543,7 +553,7 @@
             vmem((keys, size), F32),
             vmem((BLOCKS - 1, SHARE, size), BF16),
             vmem((BLOCKS - 1, SHARE, size), BF16),
-            dma((4 + 4 * HEADS,)),
+            dma((5 + 4 * HEADS,)),
             dma((RING, 3)),
             dma((2, 2)),
             dma((2, 2)),

time: 69.1 us -> 68.3 us (0.988)
  Pallas kernels: 68.1 us -> 67.4 us
    pallas_call x1, Pallas kernels: 66.3 us -> 65.5 us  [per_device(): pl.pallas_call(kernel, out_shape=outputs, in_specs=[pl.BlockSpec(memory_s...]
where the time goes in v4:
time: 68.3 us; the launch traced here: 68 us
  Pallas kernels  67.4 us (99%)
    pallas_call x1, Pallas kernels, per_device(): pl.pallas_call(kernel, out_shape=outputs, in_specs=[pl.BlockSpec(memory_s...  65.5 us
    pallas_call x1, Pallas kernels, per_device(): pl.pallas_call(finish_kernel, out_shape=outputs, in_specs=[whole] * 3, ou...  1.81 us

profile of v4, /device:TPU:1, one launch (start us, length us, event | category | flops | bytes accessed | tf_op | source)
XLA Modules:
  0.0 68.0 jit_solution(10235901582996490795)
XLA Ops:
  0.6 65.5 %shard_map.121 = (bf16[16,5120]{1,0:T(8,128)(2,1)}, bf16[512,128]{1,0:T(8,128)(2,1)}, bf16[512,128]{1,0:T(8,128)(2,1)}) custom-call(s32[16]{0:T(128)} %lengths_hbm.1, bf16[1024,128]{1,0:T(8,128)(2,1)} %bitcast.9, bf16[1024,128]{1,0:T(8,128)(2,1)} %bitcast.10, bf16[128,128]{1,0:T(8,128)(2,1)} %bitcast.13, bf16[128,128]{1,0:T(8,128)(2,1)} %bitcast.14, ...), custom_call_target="tpu_custom_call" | custom-call | tf_op jit(solution)/shard_map/pallas_call | solution.py:515
  66.2 1.8 %shard_map.122 = (bf16[16,5120]{1,0:T(8,128)(2,1)}, bf16[512,128]{1,0:T(8,128)(2,1)}, bf16[512,128]{1,0:T(8,128)(2,1)}) custom-call(bf16[16,5120]{1,0:T(8,128)(2,1)} %get-tuple-element.9.hidden_in, bf16[512,128]{1,0:T(8,128)(2,1)} %get-tuple-element.10.dk_in, bf16[512,128]{1,0:T(8,128)(2,1)} %get-tuple-element.11.dv_in), custom_call_target="tpu_custom_call" | custom-call | tf_op jit(solution)/shard_map/pallas_call | solution.py:596

commit v5 on v4

--- a/solution.py
+++ b/solution.py
@@ -388,14 +388,14 @@
                     sides.append(part.reshape(HEADS, 1, 8, narrow))
             here = pl.ds(pl.multiple_of((h * steps + t) * HEADS * 32, 32), HEADS * 32)
             q_scaled[here, :] = jnp.concatenate(sides, axis=1).reshape(HEADS * 32, narrow).astype(BF16)
-            for e in range(1, HEADS):
-                hidden_copy(h, t, e).start()
-
             @pl.when(v + RING < 4 * steps)
             def _():
                 for i in range(2):
                     for load in weight_loads(v + RING + i):
                         load.start()
+
+            for e in range(1, HEADS):
+                hidden_copy(h, t, e).start()
 
             return carry
 

time: 68.3 us -> 67.8 us (level)
  no operation moved by 1% of the time
where the time goes in v5:
time: 67.8 us; the launch traced here: 67.5 us
  Pallas kernels  66.9 us (99%)
    pallas_call x1, Pallas kernels, per_device(): pl.pallas_call(kernel, out_shape=outputs, in_specs=[pl.BlockSpec(memory_s...  65.1 us
    pallas_call x1, Pallas kernels, per_device(): pl.pallas_call(finish_kernel, out_shape=outputs, in_specs=[whole] * 3, ou...  1.81 us

profile of v5, /device:TPU:1, one launch (start us, length us, event | category | flops | bytes accessed | tf_op | source)
XLA Modules:
  0.0 67.5 jit_solution(503892680052292619)
XLA Ops:
  0.6 65.1 %shard_map.121 = (bf16[16,5120]{1,0:T(8,128)(2,1)}, bf16[512,128]{1,0:T(8,128)(2,1)}, bf16[512,128]{1,0:T(8,128)(2,1)}) custom-call(s32[16]{0:T(128)} %lengths_hbm.1, bf16[1024,128]{1,0:T(8,128)(2,1)} %bitcast.9, bf16[1024,128]{1,0:T(8,128)(2,1)} %bitcast.10, bf16[128,128]{1,0:T(8,128)(2,1)} %bitcast.13, bf16[128,128]{1,0:T(8,128)(2,1)} %bitcast.14, ...), custom_call_target="tpu_custom_call" | custom-call | tf_op jit(solution)/shard_map/pallas_call | solution.py:515
  65.7 1.8 %shard_map.122 = (bf16[16,5120]{1,0:T(8,128)(2,1)}, bf16[512,128]{1,0:T(8,128)(2,1)}, bf16[512,128]{1,0:T(8,128)(2,1)}) custom-call(bf16[16,5120]{1,0:T(8,128)(2,1)} %get-tuple-element.9.hidden_in, bf16[512,128]{1,0:T(8,128)(2,1)} %get-tuple-element.10.dk_in, bf16[512,128]{1,0:T(8,128)(2,1)} %get-tuple-element.11.dv_in), custom_call_target="tpu_custom_call" | custom-call | tf_op jit(solution)/shard_map/pallas_call | solution.py:596
